TPU v7x, 32 devices: a whole 2x2x4 slice. The times are simulated.
32 devices in a mesh: lat: 4 (over y, core), lon: 8 (over z, x).
Axes of the slice: x: 2, y: 2, z: 4, core: 2. Of those that a mesh axis runs over, the one named last changes fastest.
Arguments:
- losses: float32 [8, 16, 512, 256], P('lat', 'lon'), may hold values from -6 to 6
- positions: float32 [8, 16, 2, 512], P('lat', 'lon'), may hold values from 0 to 1
- leaf_basis: float32 [8, 16, 512, 64], P('lat', 'lon'), may hold values from -0.25 to 0.25
- near_flags: int32 [8, 16, 9], P('lat', 'lon'), may hold values from 0 to 1, as said below
- leaf_coupling: bfloat16 [8, 16, 36, 64, 64], P('lat', 'lon'), may hold values from -0.75 to 0.75
- leaf_transfer: float32 [8, 16, 64, 64], P('lat', 'lon'), may hold values from -0.75 to 0.75
- device_coupling: bfloat16 [4, 8, 36, 64, 64], P('lat', 'lon'), may hold values from -0.1875 to 0.1875
- device_transfer: float32 [4, 8, 64, 64], replicated, may hold values from -0.75 to 0.75
- group_coupling: bfloat16 [2, 4, 2, 4, 64, 64], replicated, may hold values from -0.09375 to 0.09375
Outputs:
- applied: float32 [8, 16, 512, 256], P('lat', 'lon')
Inputs may be any that keep to these rules, and one draw needn't show every extreme that they name: near_flags[i, j, 3 (di + 1) + dj + 1] is 1 when leaf (i + di, (j + dj) mod 16) forms a dense block with leaf (i, j); the flags of a pair agree seen from both leaves, the middle flag is always 1, and flags toward latitude indices outside the grid are 0.
All inputs are finite; a program needn't handle non-finite values.
Results may differ from a plain program's by a relative error of at most 0.0003.
Values sent between devices are 32-bit elements; how exact they have to be, the bound alone decides.
No kernel may reach another device: no remote copies, remote signals or barrier semaphores. Data moves between devices by JAX's collectives and lax.ppermute only.
A program may use at most 192 MiB of HBM per device.

v0:
```python
import functools

import jax
import jax.numpy as jnp
from jax import lax
from jax.experimental import pallas as pl
from jax.experimental.pallas import tpu as pltpu
from jax.sharding import PartitionSpec as P

PTS = 512
RANK = 64
COLS = 256
HALF = 256
QUAD = 4 * RANK
MSG = QUAD + 16

LN2 = 0.6931471805599453
UNIT = 1.7320508075688772 / 0.15 / LN2

f32 = jnp.float32
bf16 = jnp.bfloat16
VMEM = pltpu.VMEM
SMEM = pltpu.SMEM
whole = pl.BlockSpec(memory_space=VMEM)
scalars = pl.BlockSpec(memory_space=SMEM)


def split(x):
    hi = x.astype(bf16)
    return hi, (x - hi.astype(f32)).astype(bf16)


def mm(a, b, dims=(1, 0)):
    return lax.dot_general(
        a, b, (((dims[0],), (dims[1],)), ((), ())), preferred_element_type=f32
    )


def mm3(a, b, dims=(1, 0)):
    a_hi, a_lo = split(a)
    b_hi, b_lo = split(b)
    return mm(a_hi, b_hi, dims) + (mm(a_lo, b_hi, dims) + mm(a_hi, b_lo, dims))


def mm2(a, b):
    b_hi, b_lo = split(b)
    return mm(a, b_hi) + mm(a, b_lo)


def params(limit=24):
    return pltpu.CompilerParams(vmem_limit_bytes=limit * 1024 * 1024)


def shape(*dims):
    return jax.ShapeDtypeStruct(dims, f32)


def lat_parity():
    return lax.rem(lax.axis_index("lat"), 2)


def coef_kernel(loss, basis, transfer, pos, a_right, a_left, b_right, b_left, to_y, to_c, tpos, dev):
    parity = lat_parity()
    total = None
    for leaf in range(4):
        row, col = leaf // 2, leaf % 2
        values = loss[leaf]
        l_hi, l_lo = split(values)
        b_hi, b_lo = split(basis[leaf])
        coef = mm(b_hi, l_hi) + (mm(b_lo, l_hi) + mm(b_hi, l_lo))
        place = pos[leaf] * UNIT
        tpos[leaf] = jnp.concatenate([place, jnp.zeros((6, PTS), f32)], 0).T
        for ref, base in ((a_right, PTS), (a_left, PTS), (to_y, 2 * PTS), (to_c, 2 * PTS)):
            ref[base + leaf * RANK : base + (leaf + 1) * RANK, :] = coef
            for coord in range(2):
                for half in range(2):
                    at = base + QUAD + 4 * leaf + 2 * coord + half
                    ref[at : at + 1, :] = place[
                        coord : coord + 1, half * HALF : (half + 1) * HALF
                    ]
        part = mm3(transfer[leaf], coef, (0, 0))
        total = part if leaf == 0 else total + part

        @pl.when(parity == row)
        def _():
            (a_right if col else a_left)[:PTS, :] = values
            to_y[col * PTS : (col + 1) * PTS, :] = values

        @pl.when(parity != row)
        def _():
            (b_right if col else b_left)[...] = values
            to_c[col * PTS : (col + 1) * PTS, :] = values

    dev[...] = total


def coefficients(losses, basis, transfer, positions):
    return pl.pallas_call(
        coef_kernel,
        in_specs=[whole] * 4,
        out_specs=[whole] * 8,
        out_shape=[
            shape(PTS + MSG, COLS),
            shape(PTS + MSG, COLS),
            shape(PTS, COLS),
            shape(PTS, COLS),
            shape(2 * PTS + MSG, COLS),
            shape(2 * PTS + MSG, COLS),
            shape(4, PTS, 8),
            shape(RANK, COLS),
        ],
        compiler_params=params(16),
        cost_estimate=pl.CostEstimate(
            flops=1_000_000_000, bytes_accessed=6_000_000, transcendentals=0
        ),
        name="coefs",
    )(losses, basis, transfer, positions)


def near_scratch(n_slots, n_pairs):
    return [
        SMEM((n_pairs + 1, 8), jnp.int32),
        VMEM((n_slots, 8, PTS), f32),
        VMEM((n_slots, 2 * PTS, COLS), bf16),
        VMEM((PTS, 2 * PTS), bf16),
        VMEM((PTS, 2 * PTS), bf16),
    ]


def near_blocks(flags, tpos, slots, pairs, acc, scratch):
    table, spos, stack, kern_a, kern_b = scratch
    for slot, (values, places, base) in enumerate(slots):
        hi, lo = split(values)
        stack[slot, :PTS, :] = hi
        stack[slot, PTS:, :] = lo
        for coord in range(2):
            for half in range(2):
                spos[slot, coord : coord + 1, half * HALF : (half + 1) * HALF] = places[
                    pl.ds(base + 2 * coord + half, 1), :
                ]
    count = 0
    for slot, row, col, own_row, own_col in pairs:
        target = 2 * own_row + own_col
        table[count, 0] = slot
        table[count, 1] = target
        table[count, 2] = row - own_row
        table[count, 3] = col - own_col
        flag = flags[target, 3 * (row - own_row + 1) + col - own_col + 1]
        count = count + jnp.where(flag > 0, 1, 0)

    def evaluate(index, half, kern):
        slot, target = table[index, 0], table[index, 1]
        src_row = spos[slot, 0:1, :] + table[index, 2].astype(f32) * UNIT
        src_col = spos[slot, 1:2, :] + table[index, 3].astype(f32) * UNIT
        part = slice(half * HALF, (half + 1) * HALF)
        d_row = tpos[target, part, 0:1] - src_row
        d_col = tpos[target, part, 1:2] - src_col
        square = d_row * d_row + d_col * d_col
        dist = square * lax.rsqrt(jnp.maximum(square, 1e-30))
        decay = jnp.exp2(-dist)
        hi, lo = split(decay + decay * (dist * LN2))
        kern[part, :PTS] = hi
        kern[part, PTS:] = lo

    def apply(index, half, kern):
        slot, target = table[index, 0], table[index, 1]
        part = slice(half * HALF, (half + 1) * HALF)
        l_hi = stack[slot, :PTS, :]
        l_lo = stack[slot, PTS:, :]
        k_hi = kern[part, :PTS]
        k_lo = kern[part, PTS:]
        acc[target, part, :] += mm(k_hi, l_hi) + mm(k_lo, l_hi) + mm(k_hi, l_lo)

    def step(index, kern, other):
        following = jnp.minimum(index + 1, count - 1)
        for half in range(2):
            evaluate(following, half, other)
            apply(index, half, kern)

    @pl.when(count > 0)
    def _():
        for half in range(2):
            evaluate(0, half, kern_a)

    @pl.loop(0, (count + 1) // 2)
    def _(pair):
        step(2 * pair, kern_a, kern_b)

        @pl.when(2 * pair + 1 < count)
        def _():
            step(2 * pair + 1, kern_b, kern_a)


def near_cost(n_pairs):
    return pl.CostEstimate(
        flops=n_pairs * 500_000_000,
        bytes_accessed=4_000_000,
        transcendentals=n_pairs * 2 * PTS * PTS,
    )


ACC = shape(4, PTS, COLS)


def own_kernel(flags, tpos, loss, msg, acc, *scratch):
    slots = [(loss[leaf], msg, PTS + QUAD + 4 * leaf) for leaf in range(4)]
    pairs = [(s, s // 2, s % 2, t // 2, t % 2) for s in range(4) for t in range(4)]
    for leaf in range(4):
        acc[leaf] = 0.5 * loss[leaf]
    near_blocks(flags, tpos, slots, pairs, acc, scratch)


def lat_kernel(flags, tpos, from_y, from_c, before, acc, *scratch):
    acc[...] = before[...]
    parity = lat_parity()
    base = 2 * PTS + QUAD
    slots, pairs = [], []
    for ref, place, row, own_row in (
        (from_y, 8 - 8 * parity, 3 * parity - 1, parity),
        (from_c, 8 * parity, 2 - 3 * parity, 1 - parity),
    ):
        for col in range(2):
            for own_col in range(2):
                pairs.append((len(slots), row, col, own_row, own_col))
            slots.append((ref[col * PTS : (col + 1) * PTS, :], ref, base + place + 4 * col))
    near_blocks(flags, tpos, slots, pairs, acc, scratch)


def lon_kernel(flags, tpos, left, right, before, acc, to_c, *scratch):
    acc[...] = before[...]
    parity = lat_parity()
    to_c[:QUAD, :] = left[PTS : PTS + QUAD, :]
    to_c[QUAD : 2 * QUAD, :] = right[PTS : PTS + QUAD, :]
    to_c[2 * QUAD : 2 * QUAD + 16, :] = left[PTS + QUAD :, :]
    to_c[2 * QUAD + 16 :, :] = right[PTS + QUAD :, :]
    base = PTS + QUAD + 8 * parity
    slots = [(left[:PTS, :], left, base + 4), (right[:PTS, :], right, base)]
    pairs = [(s, parity, 3 * s - 1, i, s) for s in range(2) for i in range(2)]
    near_blocks(flags, tpos, slots, pairs, acc, scratch)


def last_kernel(flags, tpos, a_left, a_right, left, right, c_ends, left_c, right_c, before, acc, *scratch):
    acc[...] = before[...]
    parity = lat_parity()
    base = PTS + QUAD + 8 - 8 * parity
    ends = 2 * QUAD + 8 * parity
    slots = [
        (left[...], a_left, base + 4),
        (right[...], a_right, base),
        (left_c[...], c_ends, ends + 4),
        (right_c[...], c_ends, ends + 16),
    ]
    pairs = [(s, 1 - parity, 3 * s - 1, i, s) for s in range(2) for i in range(2)]
    pairs += [(2 + s, 2 - 3 * parity, 3 * s - 1, 1 - parity, s) for s in range(2)]
    near_blocks(flags, tpos, slots, pairs, acc, scratch)


def near(kernel, name, n_slots, n_pairs, operands, more=(), chained=True):
    return pl.pallas_call(
        kernel,
        in_specs=[scalars] + [whole] * (len(operands) - 1),
        out_specs=[whole] * (1 + len(more)),
        out_shape=[ACC, *more],
        scratch_shapes=near_scratch(n_slots, n_pairs),
        input_output_aliases={len(operands) - 1: 0} if chained else {},
        compiler_params=params(),
        cost_estimate=near_cost(n_pairs),
        name=name,
    )(*operands)


def window_sum(flags, weights, bands):
    total = None
    for base, cells in bands:
        for v in range(6):
            if cells[v // 2] is None:
                continue
            ref, offset = cells[v // 2]
            for a in range(2):
                start = offset + (2 * a + v % 2) * RANK
                hi, lo = split(ref[start : start + RANK, :])
                u = base + a
                w = 6 * u + v
                rows = []
                for leaf in range(4):
                    block = weights[leaf, w]
                    d_row = u - 2 - leaf // 2
                    d_col = v - 2 - leaf % 2
                    if abs(d_col) <= 1:
                        inside = (d_row >= -1) & (d_row <= 1)
                        flag = flags[leaf, 3 * jnp.clip(d_row + 1, 0, 2) + d_col + 1]
                        keep = 1 - jnp.where(inside, flag, 0)
                        block = (block.astype(f32) * keep.astype(f32)).astype(bf16)
                    rows.append(block)
                stacked = jnp.concatenate(rows, 0)
                part = mm(stacked, hi) + mm(stacked, lo)
                total = part if total is None else total + part
    return total


def far_kernel(
    n_lat, n_lon, flags, weights, own, left, right, from_y, from_c, every, dev_w, dev_t, group_w,
    leaf_t, out, group_row_w,
):
    lat = lax.axis_index("lat")
    lon = lax.axis_index("lon")
    parity = lax.rem(lat, 2)
    group_row, group_col = lat // 2, lon // 2
    n_gcol = n_lon // 2
    pltpu.sync_copy(group_w.at[group_row, group_col], group_row_w)
    total = jnp.zeros((RANK, COLS), f32)
    for other in range(n_lat):
        u = other + 2 - 2 * group_row
        for v in range(6):
            shift = 2 * group_col - 2 + v
            col = lax.rem(shift + n_lon, n_lon)
            drop = (jnp.abs(other - lat) <= 1) & (jnp.abs(shift - lon) <= 1)
            scale = jnp.where(drop, 0.0, 1.0)
            total = total + scale * mm2(dev_w[6 * u + v], every[other * n_lon + col])

    def group_step(step, field):
        gcol = lax.rem(group_col + step, n_gcol)
        for grow in range(n_lat // 2):
            coef = jnp.zeros((RANK, COLS), f32)
            for e in range(2):
                for f in range(2):
                    cell = (2 * grow + e) * n_lon + 2 * gcol + f
                    coef = coef + mm3(dev_t[cell], every[cell], (0, 0))
            field = field + mm2(group_row_w[grow, gcol], coef)
        return field

    field = lax.fori_loop(2, n_gcol - 1, group_step, jnp.zeros((RANK, COLS), f32))
    total = total + mm3(dev_t[lat * n_lon + lon], field)
    far = window_sum(
        flags,
        weights,
        (
            (2, ((left, PTS), (own, PTS), (right, PTS))),
            (4 * parity, (None, (from_y, 2 * PTS), None)),
            (4 - 4 * parity, (None, (from_c, 2 * PTS), None)),
        ),
    )
    for leaf in range(4):
        rows = slice(leaf * RANK, (leaf + 1) * RANK)
        out[rows, :] = far[rows, :] + mm3(leaf_t[leaf], total)


def far_field(n_lat, n_lon, operands):
    specs = [scalars] + [whole] * 11
    specs[10] = pl.BlockSpec(memory_space=pl.ANY)
    return pl.pallas_call(
        functools.partial(far_kernel, n_lat, n_lon),
        in_specs=specs,
        out_specs=whole,
        out_shape=shape(QUAD, COLS),
        scratch_shapes=[VMEM((n_lat // 2, n_lon // 2, RANK, RANK), bf16)],
        compiler_params=params(),
        cost_estimate=pl.CostEstimate(
            flops=6_000_000_000, bytes_accessed=9_000_000, transcendentals=0
        ),
        name="far",
    )(*operands)


def down_kernel(
    flags, tpos, weights, left_y, right_y, c_ends, partial, basis, before, acc, *scratch
):
    acc[...] = before[...]
    parity = lat_parity()
    far = partial[...] + window_sum(
        flags,
        weights,
        (
            (4 * parity, ((left_y, PTS), None, (right_y, PTS))),
            (4 - 4 * parity, ((c_ends, 0), None, (c_ends, QUAD))),
        ),
    )
    for leaf in range(4):
        acc[leaf] += mm3(basis[leaf], far[leaf * RANK : (leaf + 1) * RANK, :], (0, 0))
    base = PTS + QUAD + 8 - 8 * parity
    slots = [(left_y[:PTS, :], left_y, base + 4), (right_y[:PTS, :], right_y, base)]
    pairs = [(s, 3 * parity - 1, 3 * s - 1, parity, s) for s in range(2)]
    near_blocks(flags, tpos, slots, pairs, acc, scratch)


def local(
    losses,
    positions,
    leaf_basis,
    near_flags,
    leaf_coupling,
    leaf_transfer,
    device_coupling,
    device_transfer,
    group_coupling,
):
    n_lat = lax.axis_size("lat")
    n_lon = lax.axis_size("lon")

    flat = losses.reshape(4, PTS, COLS)
    basis = jnp.swapaxes(leaf_basis, 2, 3).reshape(4, RANK, PTS)
    flags = near_flags.reshape(4, 9)
    weights = leaf_coupling.reshape(4, 36, RANK, RANK)
    transfer = leaf_transfer.reshape(4, RANK, RANK)

    to_right = [(i, (i + 1) % n_lon) for i in range(n_lon)]
    to_left = [(i, (i - 1) % n_lon) for i in range(n_lon)]
    in_chip = [(i, i ^ 1) for i in range(n_lat)]
    across = [(i, i + 1 if i % 2 else i - 1) for i in range(n_lat)]
    across = [(a, b) for a, b in across if 0 <= b < n_lat]

    a_right, a_left, b_right, b_left, to_y, to_c, tpos, dev = coefficients(
        flat, basis, transfer, positions.reshape(4, 2, PTS)
    )
    left = lax.ppermute(a_right, "lon", to_right)
    right = lax.ppermute(a_left, "lon", to_left)
    from_c = lax.ppermute(to_c, "lat", in_chip)
    left_b = lax.ppermute(b_right, "lon", to_right)
    right_b = lax.ppermute(b_left, "lon", to_left)
    from_y = lax.ppermute(to_y, "lat", across)

    pairs = [[2 * k, 2 * k + 1] for k in range(n_lon // 2)]
    classes = [list(range(j, n_lon, 2)) for j in range(2)]
    every = lax.all_gather(dev, "lon", axis_index_groups=pairs)
    every = lax.all_gather(every, "lon", axis_index_groups=classes)
    every = lax.all_gather(every, "lat")
    every = every.reshape(n_lat * n_lon, RANK, COLS)

    (acc,) = near(own_kernel, "own", 4, 16, (flags, tpos, flat, a_right), chained=False)
    (acc,) = near(lat_kernel, "lat", 4, 8, (flags, tpos, from_y, from_c, acc))
    left, right, acc = lax.optimization_barrier((left, right, acc))
    left_y = lax.ppermute(left, "lat", across)
    right_y = lax.ppermute(right, "lat", across)
    acc, to_c = near(
        lon_kernel, "lon", 2, 4, (flags, tpos, left, right, acc), more=[shape(2 * MSG, COLS)]
    )
    c_ends = lax.ppermute(to_c, "lat", in_chip)
    partial = far_field(
        n_lat,
        n_lon,
        (
            flags,
            weights,
            a_right,
            left,
            right,
            from_y,
            from_c,
            every,
            device_coupling.reshape(36, RANK, RANK),
            device_transfer.reshape(n_lat * n_lon, RANK, RANK),
            group_coupling,
            transfer,
        ),
    )
    left_c = lax.ppermute(left_b, "lat", in_chip)
    right_c = lax.ppermute(right_b, "lat", in_chip)
    (acc,) = near(
        down_kernel,
        "down",
        2,
        2,
        (flags, tpos, weights, left_y, right_y, c_ends, partial, basis, acc),
    )
    (acc,) = near(
        last_kernel,
        "last",
        4,
        6,
        (flags, tpos, left, right, left_b, right_b, c_ends, left_c, right_c, acc),
    )
    return acc.reshape(2, 2, PTS, COLS)


def solution(mesh):
    placed = (
        P("lat", "lon", None, None),
        P("lat", "lon", None, None),
        P("lat", "lon", None, None),
        P("lat", "lon", None),
        P("lat", "lon", None, None, None),
        P("lat", "lon", None, None),
        P("lat", "lon", None, None, None),
        P(),
        P(),
    )
    return jax.shard_map(
        local, mesh=mesh, in_specs=placed, out_specs=P("lat", "lon", None, None), check_vma=False
    )
```

profile of v0, /device:TPU:9, one launch (start us, length us, event | category | flops | bytes accessed | tf_op | source)
XLA Modules:
  0.0 147.2 jit_solution(14027102786052563266)
XLA Ops:
  6.5 1.0 copy-done.1
  7.6 1.6 %copy-done.4 = f32[2,2,512,256]{3,2,1,0:T(8,128)S(1)} copy-done((f32[2,2,512,256]{3,2,1,0:T(8,128)S(1)}, f32[2,2,512,256]{3,2,1,0:T(8,128)}, u32[]{:S(2)}) %copy-start.4) | copy-done | bytes 2097176
  10.8 1.9 %coefs.1 = (f32[784,256]{1,0:T(8,128)S(1)}, f32[784,256]{1,0:T(8,128)S(1)}, f32[512,256]{1,0:T(8,128)S(1)}, f32[512,256]{1,0:T(8,128)S(1)}, f32[1296,256]{1,0:T(...) custom-call(f32[4,512,256]{2,1,0:T(8,128)S(1)} %bitcast.24, ...), custom_call_target="tpu_custom_call" | custom-call | flops 1000000000 | bytes 6000000 | tf_op jit(solution)/shard_map/coefs/pallas_call | solution.py:98
  12.7 1.0 copy-done.11
  13.7 1.1 copy-done.12
  18.2 3.8 %all-gather = f32[128,256]{1,0:T(8,128)S(1)} all-gather(f32[64,256]{1,0:T(8,128)S(1)} %get-tuple-element.29), channel_id=2, replica_groups={{0,1},{2,3},{4,5},{6,7},{8,9},{10,11},{12,13},{14,15},{16,17},{18,19},{..., dimensions={0}, use_global_device_ids=true | all-gather | bytes 196608 | tf_op jit(solution)/shard_map/all_gather | solution.py:424
  22.0 12.9 %all-gather.1 = f32[8,64,256]{2,1,0:T(8,128)} all-gather(f32[2,64,256]{2,1,0:T(8,128)S(1)} %bitcast.33), channel_id=3, replica_groups={{0,2,4,6},{1,3,5,7},{8,10,12,14},{9,11,13,15},{16,18,20,22},{17,19,21,2..., dimensions={0}, use_global_device_ids=true | all-gather | bytes 655360 | tf_op jit(solution)/shard_map/all_gather | solution.py:425
  34.9 8.4 %collective-permute-start.2 = (f32[1296,256]{1,0:T(8,128)}, f32[1296,256]{1,0:T(8,128)S(1)}, u32[]{:S(2)}, u32[]{:S(2)}) collective-permute-start(f32[1296,256]{1,0:T(8,128)} %copy-done.12), channel_id=1, source_target_pairs={{8,16},{16,8},{9,17},{17,9},{10,18},{18,10},{11,19},{19,11},{12,20... | collective-permute-start | bytes 3981320 | tf_op jit(solution)/shard_map/ppermute | solution.py:420
  43.4 1.3 collective-permute-start
  44.6 1.2 collective-permute-start.1
  46.1 24.5 %collective-permute-done.2.from_y = f32[1296,256]{1,0:T(8,128)S(1)} collective-permute-done((f32[1296,256]{1,0:T(8,128)}, f32[1296,256]{1,0:T(8,128)S(1)}, u32[]{:S(2)}, u32[]{:S(2)}) %collective-permute-start.2) | collective-permute-done | bytes 1327136 | tf_op jit(solution)/shard_map/ppermute | solution.py:420
  71.1 1.1 copy-done.16
  72.3 6.7 %own.1.before = f32[4,512,256]{2,1,0:T(8,128)} custom-call(s32[4,9]{1,0:T(4,128)S(1)} %bitcast.18, f32[4,512,8]{2,1,0:T(8,128)S(1)} %get-tuple-element.18.tpos, f32[4,512,256]{2,1,0:T(8,128)S(1)} %bitcast.25, f32[784,256]{1,0:T(8,128)S(1)} %copy-done.16), custom_call_target="tpu_custom_call" | custom-call | flops 8000000000 | bytes 4000000 | tf_op jit(solution)/shard_map/own/pallas_call | solution.py:259
  78.9 6.4 %lat.1.before = f32[4,512,256]{2,1,0:T(8,128)} custom-call(s32[4,9]{1,0:T(4,128)S(1)} %bitcast.19, f32[4,512,8]{2,1,0:T(8,128)S(1)} %get-tuple-element.18.tpos, f32[1296,256]{1,0:T(8,128)S(1)} %collective-permute-done.2.from_y, f32[1296,256]{1,0:T(8,128)S(1)} %collective-permute-done.3.from_c, f32[4,512,256]{2,1,0:T(8,128)} %own.1.before), custom_call_target="tpu_custom_call", output_to_operand_aliasing={{}: (4, {})} | custom-call | flops 4000000000 | bytes 4000000 | tf_op jit(solution)/shard_map/lat/pallas_call | solution.py:259
  85.4 4.9 %collective-permute-done.left.a_left = f32[784,256]{1,0:T(8,128)} collective-permute-done((f32[784,256]{1,0:T(8,128)}, f32[784,256]{1,0:T(8,128)}, u32[]{:S(2)}, u32[]{:S(2)}) %collective-permute-start) | collective-permute-done | bytes 802848 | tf_op jit(solution)/shard_map/ppermute | solution.py:415
  90.2 2.7 %collective-permute-done.1.right.a_right = f32[784,256]{1,0:T(8,128)} collective-permute-done((f32[784,256]{1,0:T(8,128)}, f32[784,256]{1,0:T(8,128)}, u32[]{:S(2)}, u32[]{:S(2)}) %collective-permute-start.1) | collective-permute-done | bytes 802848 | tf_op jit(solution)/shard_map/ppermute | solution.py:416
  92.9 2.4 %collective-permute-start.10 = (f32[784,256]{1,0:T(8,128)}, f32[784,256]{1,0:T(8,128)}, u32[]{:S(2)}, u32[]{:S(2)}) collective-permute-start(f32[784,256]{1,0:T(8,128)} %collective-permute-done.1.right.a_right), channel_id=1, source_target_pairs={{8,16},{16,8},{9,17},{17,9},{10,18},{18,10},{11,19},{19,11},{12,20... | collective-permute-start | bytes 2408456 | tf_op jit(solution)/shard_map/ppermute | solution.py:433
  95.3 3.1 %collective-permute-start.9 = (f32[784,256]{1,0:T(8,128)}, f32[784,256]{1,0:T(8,128)}, u32[]{:S(2)}, u32[]{:S(2)}) collective-permute-start(f32[784,256]{1,0:T(8,128)} %collective-permute-done.left.a_left), channel_id=1, source_target_pairs={{8,16},{16,8},{9,17},{17,9},{10,18},{18,10},{11,19},{19,11},{12,20... | collective-permute-start | bytes 2408456 | tf_op jit(solution)/shard_map/ppermute | solution.py:432
  98.5 3.0 %collective-permute-done.4.left = f32[512,256]{1,0:T(8,128)} collective-permute-done((f32[512,256]{1,0:T(8,128)}, f32[512,256]{1,0:T(8,128)}, u32[]{:S(2)}, u32[]{:S(2)}) %collective-permute-start.4) | collective-permute-done | bytes 524320 | tf_op jit(solution)/shard_map/ppermute | solution.py:418
  101.4 1.3 collective-permute-start.7
  102.7 1.4 collective-permute-done.5.right
  104.6 8.4 %lon.1 = (f32[4,512,256]{2,1,0:T(8,128)}, f32[544,256]{1,0:T(8,128)}) custom-call(s32[4,9]{1,0:T(4,128)S(1)} %bitcast.20, f32[4,512,8]{2,1,0:T(8,128)S(1)} %get-tuple-element.18.tpos, f32[784,256]{1,0:T(8,128)} %collective-permute-done.left.a_left, f32[784,256]{1,0:T(8,128)} %collective-permute-done.1.right.a_right, ...), custom_call_target="tpu_custom_call", output_to_operand_aliasing={{0}: (4, {})} | custom-call | flops 2000000000 | bytes 4000000 | tf_op jit(solution)/shard_map/lon/pallas_call | solution.py:259
  113.0 1.6 %copy-done.6 = f32[16,2,64,256]{3,2,1,0:T(8,128)S(1)} copy-done((f32[16,2,64,256]{3,2,1,0:T(8,128)S(1)}, f32[16,2,64,256]{3,2,1,0:T(8,128)}, u32[]{:S(2)}) %copy-start.6) | copy-done | bytes 2097176
  114.6 1.3 copy-done.8
  116.0 1.3 copy-done.10
  117.3 1.2 copy-done.13
  118.5 1.2 copy-done.14
  119.7 1.1 copy-done.17
  120.9 1.1 copy-done.19
  121.9 4.6 %far.1.partial = f32[256,256]{1,0:T(8,128)S(1)} custom-call(s32[4,9]{1,0:T(4,128)S(1)} %bitcast.21, bf16[4,36,64,64]{3,2,1,0:T(8,128)(2,1)S(1)} %bitcast.14, f32[784,256]{1,0:T(8,128)S(1)} %copy-done.17, f32[784,256]{1,0:T(8,128)} %collective-permute-done.left.a_left, f32[784,256]{1,0:T(8,128)} %collective-permute-done.1.right.a_right, ...), custom_call_target="tpu_custom_call" | custom-call | flops 6000000000 | bytes 9000000 | tf_op jit(solution)/shard_map/far/pallas_call | solution.py:351
  126.5 7.5 %down.1.before = f32[4,512,256]{2,1,0:T(8,128)} custom-call(s32[4,9]{1,0:T(4,128)S(1)} %bitcast.22, f32[4,512,8]{2,1,0:T(8,128)S(1)} %get-tuple-element.18.tpos, bf16[4,36,64,64]{3,2,1,0:T(8,128)(2,1)S(1)} %bitcast.15, f32[784,256]{1,0:T(8,128)} %collective-permute-done.9.left_y, ...), custom_call_target="tpu_custom_call", output_to_operand_aliasing={{}: (8, {})} | custom-call | flops 1000000000 | bytes 4000000 | tf_op jit(solution)/shard_map/down/pallas_call | solution.py:259
  134.1 6.3 %last.1 = f32[4,512,256]{2,1,0:T(8,128)} custom-call(s32[4,9]{1,0:T(4,128)S(1)} %bitcast.23, f32[4,512,8]{2,1,0:T(8,128)S(1)} %get-tuple-element.18.tpos, f32[784,256]{1,0:T(8,128)} %collective-permute-done.left.a_left, f32[784,256]{1,0:T(8,128)} %collective-permute-done.1.right.a_right, ...), custom_call_target="tpu_custom_call", output_to_operand_aliasing={{}: (9, {})} | custom-call | flops 3000000000 | bytes 4000000 | tf_op jit(solution)/shard_map/last/pallas_call | solution.py:259
  (52 shorter events, 6.6 us)
Async XLA Ops:
  6.5 106.5 %all-gather.5.cloned.1.call-start = ((), (), s32[]{:S(2)}) async-start(), calls=%async_computation | async-start | bytes 2621440 | tf_op jit(solution)/shard_map/all_gather | solution.py:426
  6.5 1.0 copy-start.1
  7.6 1.6 %copy-start.4 = (f32[2,2,512,256]{3,2,1,0:T(8,128)S(1)}, f32[2,2,512,256]{3,2,1,0:T(8,128)}, u32[]{:S(2)}) copy-start(f32[2,2,512,256]{3,2,1,0:T(8,128)} %param.9) | copy-start | bytes 6291460
  10.8 60.3 %copy-start.3 = (s32[2,2,9]{2,1,0:T(2,128)S(1)}, s32[2,2,9]{2,1,0:T(2,128)}, u32[]{:S(2)}) copy-start(s32[2,2,9]{2,1,0:T(2,128)} %param.12) | copy-start | bytes 436
  10.8 60.3 %copy-start.5 = (f32[2,2,512,256]{3,2,1,0:T(8,128)S(1)}, f32[2,2,512,256]{3,2,1,0:T(8,128)}, u32[]{:S(2)}) copy-start(f32[2,2,512,256]{3,2,1,0:T(8,128)} %param.9) | copy-start | bytes 6291460
  12.7 1.1 copy-start.11
  13.7 1.1 copy-start.12
  15.7 0.9 copy-start.18
  34.9 35.7 %collective-permute-start.2 = (f32[1296,256]{1,0:T(8,128)}, f32[1296,256]{1,0:T(8,128)S(1)}, u32[]{:S(2)}, u32[]{:S(2)}) collective-permute-start(f32[1296,256]{1,0:T(8,128)} %copy-done.12), channel_id=1, source_target_pairs={{8,16},{16,8},{9,17},{17,9},{10,18},{18,10},{11,19},{19,11},{12,20... | collective-permute-start | bytes 3981320 | tf_op jit(solution)/shard_map/ppermute | solution.py:420
  43.3 35.7 %collective-permute-start.3 = (f32[1296,256]{1,0:T(8,128)}, f32[1296,256]{1,0:T(8,128)S(1)}, u32[]{:S(2)}, u32[]{:S(2)}) collective-permute-start(f32[1296,256]{1,0:T(8,128)} %copy-done.11), channel_id=1, source_target_pairs={{0,8},{8,0},{16,24},{24,16},{1,9},{9,1},{17,25},{25,17},{2,10},{10... | collective-permute-start | bytes 3981320 | tf_op jit(solution)/shard_map/ppermute | solution.py:417
  43.4 46.8 %collective-permute-start = (f32[784,256]{1,0:T(8,128)}, f32[784,256]{1,0:T(8,128)}, u32[]{:S(2)}, u32[]{:S(2)}) collective-permute-start(f32[784,256]{1,0:T(8,128)} %copy-done.15), channel_id=1, source_target_pairs={{0,1},{1,2},{2,3},{3,4},{4,5},{5,6},{6,7},{7,0},{8,9},{9,10},{10,1... | collective-permute-start | bytes 2408456 | tf_op jit(solution)/shard_map/ppermute | solution.py:415
  44.6 48.3 %collective-permute-start.1 = (f32[784,256]{1,0:T(8,128)}, f32[784,256]{1,0:T(8,128)}, u32[]{:S(2)}, u32[]{:S(2)}) collective-permute-start(f32[784,256]{1,0:T(8,128)} %copy-done.18), channel_id=1, source_target_pairs={{0,7},{1,0},{2,1},{3,2},{4,3},{5,4},{6,5},{7,6},{8,15},{9,8},{10,9... | collective-permute-start | bytes 2408456 | tf_op jit(solution)/shard_map/ppermute | solution.py:416
  45.8 55.7 %collective-permute-start.4 = (f32[512,256]{1,0:T(8,128)}, f32[512,256]{1,0:T(8,128)}, u32[]{:S(2)}, u32[]{:S(2)}) collective-permute-start(f32[512,256]{1,0:T(8,128)} %copy-done.21), channel_id=1, source_target_pairs={{0,1},{1,2},{2,3},{3,4},{4,5},{5,6},{6,7},{7,0},{8,9},{9,10},{10,1... | collective-permute-start | bytes 1572872 | tf_op jit(solution)/shard_map/ppermute | solution.py:418
  70.6 8.4 %copy-start.7 = (f32[1296,256]{1,0:T(8,128)}, f32[1296,256]{1,0:T(8,128)S(1)}, u32[]{:S(2)}) copy-start(f32[1296,256]{1,0:T(8,128)S(1)} %collective-permute-done.2.from_y) | copy-start | bytes 3981316
  70.6 33.5 %collective-permute-start.5 = (f32[512,256]{1,0:T(8,128)}, f32[512,256]{1,0:T(8,128)}, u32[]{:S(2)}, u32[]{:S(2)}) collective-permute-start(f32[512,256]{1,0:T(8,128)} %copy-done.20), channel_id=1, source_target_pairs={{0,7},{1,0},{2,1},{3,2},{4,3},{5,4},{6,5},{7,6},{8,15},{9,8},{10,9... | collective-permute-start | bytes 1572872 | tf_op jit(solution)/shard_map/ppermute | solution.py:419
  71.1 1.1 copy-start.16
  78.9 6.4 %copy-start.9 = (f32[1296,256]{1,0:T(8,128)}, f32[1296,256]{1,0:T(8,128)S(1)}, u32[]{:S(2)}) copy-start(f32[1296,256]{1,0:T(8,128)S(1)} %collective-permute-done.3.from_c) | copy-start | bytes 3981316
  85.4 27.7 %copy-start = (bf16[2,2,36,64,64]{4,3,2,1,0:T(8,128)(2,1)S(1)}, bf16[2,2,36,64,64]{4,3,2,1,0:T(8,128)(2,1)}, u32[]{:S(2)}) copy-start(bf16[2,2,36,64,64]{4,3,2,1,0:T(8,128)(2,1)} %param.13) | copy-start | bytes 3538948
  85.4 27.7 %copy-start.23 = (f32[2,2,64,64]{3,2,1,0:T(8,128)S(1)}, f32[2,2,64,64]{3,2,1,0:T(8,128)}, u32[]{:S(2)}) copy-start(f32[2,2,64,64]{3,2,1,0:T(8,128)} %param.14) | copy-start | bytes 196612
  92.9 33.6 %collective-permute-start.10 = (f32[784,256]{1,0:T(8,128)}, f32[784,256]{1,0:T(8,128)}, u32[]{:S(2)}, u32[]{:S(2)}) collective-permute-start(f32[784,256]{1,0:T(8,128)} %collective-permute-done.1.right.a_right), channel_id=1, source_target_pairs={{8,16},{16,8},{9,17},{17,9},{10,18},{18,10},{11,19},{19,11},{12,20... | collective-permute-start | bytes 2408456 | tf_op jit(solution)/shard_map/ppermute | solution.py:433
  95.3 31.2 %collective-permute-start.9 = (f32[784,256]{1,0:T(8,128)}, f32[784,256]{1,0:T(8,128)}, u32[]{:S(2)}, u32[]{:S(2)}) collective-permute-start(f32[784,256]{1,0:T(8,128)} %collective-permute-done.left.a_left), channel_id=1, source_target_pairs={{8,16},{16,8},{9,17},{17,9},{10,18},{18,10},{11,19},{19,11},{12,20... | collective-permute-start | bytes 2408456 | tf_op jit(solution)/shard_map/ppermute | solution.py:432
  101.4 32.6 %collective-permute-start.7 = (f32[512,256]{1,0:T(8,128)}, f32[512,256]{1,0:T(8,128)}, u32[]{:S(2)}, u32[]{:S(2)}) collective-permute-start(f32[512,256]{1,0:T(8,128)} %collective-permute-done.4.left), channel_id=1, source_target_pairs={{0,8},{8,0},{16,24},{24,16},{1,9},{9,1},{17,25},{25,17},{2,10},{10... | collective-permute-start | bytes 1572872 | tf_op jit(solution)/shard_map/ppermute | solution.py:456
  104.1 30.0 %collective-permute-start.8 = (f32[512,256]{1,0:T(8,128)}, f32[512,256]{1,0:T(8,128)}, u32[]{:S(2)}, u32[]{:S(2)}) collective-permute-start(f32[512,256]{1,0:T(8,128)} %collective-permute-done.5.right), channel_id=1, source_target_pairs={{0,8},{8,0},{16,24},{24,16},{1,9},{9,1},{17,25},{25,17},{2,10},{10... | collective-permute-start | bytes 1572872 | tf_op jit(solution)/shard_map/ppermute | solution.py:457
  113.0 13.5 %collective-permute-start.6 = (f32[544,256]{1,0:T(8,128)}, f32[544,256]{1,0:T(8,128)}, u32[]{:S(2)}, u32[]{:S(2)}) collective-permute-start(f32[544,256]{1,0:T(8,128)} %get-tuple-element.28), channel_id=1, source_target_pairs={{0,8},{8,0},{16,24},{24,16},{1,9},{9,1},{17,25},{25,17},{2,10},{10... | collective-permute-start | bytes 1671176 | tf_op jit(solution)/shard_map/ppermute | solution.py:437
  113.0 1.6 %copy-start.6 = (f32[16,2,64,256]{3,2,1,0:T(8,128)S(1)}, f32[16,2,64,256]{3,2,1,0:T(8,128)}, u32[]{:S(2)}) copy-start(f32[16,2,64,256]{3,2,1,0:T(8,128)} %all-gather.5.cloned.1.call-done) | copy-start | bytes 6291460
  114.6 1.3 copy-start.8
  116.0 1.3 copy-start.10
  117.3 1.2 copy-start.13
  118.5 1.2 copy-start.14
  119.7 1.1 copy-start.17
  120.9 1.1 copy-start.19
  121.9 4.6 %copy-start.2 = (f32[2,2,512,64]{2,3,1,0:T(8,128)S(1)}, f32[2,2,512,64]{2,3,1,0:T(8,128)}, u32[]{:S(2)}) copy-start(f32[2,2,512,64]{2,3,1,0:T(8,128)} %param.11) | copy-start | bytes 1572868
  (5 other events, 4.1 us)
Sparse Core Ops, SparseCore 0:
  35.0 34.4 all-gather.4
where the time goes:
time: 149 us; the launch traced here: 147 us
  Pallas kernels  41.7 us (28%)
  waiting for transfers between devices  36.4 us (24%)
  local copies, waits for them, and re-layouts  19.8 us (13%)
  starting transfers between devices  19 us (13%)
  blocking collectives  16.7 us (11%)
  between operations  13.5 us (9%)
    pallas_call x5, Pallas kernels, near(): pl.pallas_call(kernel, in_specs=[scalars] + [whole] * (len(operands) - 1)...  35.3 us
    ppermute x1, waiting for transfers between devices, local(): from_y = lax.ppermute(to_y, 'lat', across)  24.5 us
    unnamed x50, local copies, waits for them, and re-layouts  19.8 us
    all_gather x1, blocking collectives, local(): every = lax.all_gather(every, 'lon', axis_index_groups=classes)  12.9 us
    ppermute x1, starting transfers between devices, local(): from_y = lax.ppermute(to_y, 'lat', across)  8.37 us
    ppermute x1, waiting for transfers between devices, local(): left = lax.ppermute(a_right, 'lon', to_right)  4.85 us
    pallas_call x1, Pallas kernels, far_field(): pl.pallas_call(functools.partial(far_kernel, n_lat, n_lon), in_specs=spec...  4.55 us
    all_gather x1, blocking collectives, local(): every = lax.all_gather(dev, 'lon', axis_index_groups=pairs)  3.78 us
  transfers between devices with their start and end apart: 12, of which 5 were waited for; matrix products, arithmetic and copies ran while one was open for 0% of the time, Pallas kernels for 23%

commit v1 on v0

--- a/solution.py
+++ b/solution.py
@@ -47,7 +47,7 @@
     return mm(a, b_hi) + mm(a, b_lo)
 
 
-def params(limit=24):
+def params(limit=64):
     return pltpu.CompilerParams(vmem_limit_bytes=limit * 1024 * 1024)
 
 
@@ -59,46 +59,71 @@
     return lax.rem(lax.axis_index("lat"), 2)
 
 
-def coef_kernel(loss, basis, transfer, pos, a_right, a_left, b_right, b_left, to_y, to_c, tpos, dev):
+def coef_kernel(
+    loss, basis, transfer, pos, a_right, a_left, b_right, b_left, to_y, to_c, tpos, dev,
+    values, bases, message, sems, load_sems,
+):
     parity = lat_parity()
+    loads = []
+    for leaf in range(4):
+        loads.append(
+            (
+                pltpu.make_async_copy(loss.at[leaf], values.at[leaf], load_sems.at[leaf]),
+                pltpu.make_async_copy(basis.at[leaf], bases.at[leaf], load_sems.at[4 + leaf]),
+            )
+        )
+        for copy in loads[-1]:
+            copy.start()
+    y_row, c_row = 2 * parity, 2 - 2 * parity
+    first, second = slice(0, PTS), slice(PTS, 2 * PTS)
+    copies = []
+    for source, target in (
+        (y_row + 1, a_right.at[first]),
+        (y_row, a_left.at[first]),
+        (c_row + 1, b_right),
+        (c_row, b_left),
+        (y_row, to_y.at[first]),
+        (y_row + 1, to_y.at[second]),
+        (c_row, to_c.at[first]),
+        (c_row + 1, to_c.at[second]),
+    ):
+        copy = pltpu.make_async_copy(loss.at[source], target, sems.at[len(copies)])
+        copy.start()
+        copies.append(copy)
+    for leaf in range(4):
+        place = pos[leaf] * UNIT
+        tpos[leaf] = jnp.concatenate([place, jnp.zeros((6, PTS), f32)], 0).T
+        for coord in range(2):
+            for half in range(2):
+                at = QUAD + 4 * leaf + 2 * coord + half
+                message[at : at + 1, :] = place[coord : coord + 1, half * HALF : (half + 1) * HALF]
     total = None
     for leaf in range(4):
-        row, col = leaf // 2, leaf % 2
-        values = loss[leaf]
-        l_hi, l_lo = split(values)
-        b_hi, b_lo = split(basis[leaf])
+        for copy in loads[leaf]:
+            copy.wait()
+        l_hi, l_lo = split(values[leaf])
+        b_hi, b_lo = split(bases[leaf])
         coef = mm(b_hi, l_hi) + (mm(b_lo, l_hi) + mm(b_hi, l_lo))
-        place = pos[leaf] * UNIT
-        tpos[leaf] = jnp.concatenate([place, jnp.zeros((6, PTS), f32)], 0).T
-        for ref, base in ((a_right, PTS), (a_left, PTS), (to_y, 2 * PTS), (to_c, 2 * PTS)):
-            ref[base + leaf * RANK : base + (leaf + 1) * RANK, :] = coef
-            for coord in range(2):
-                for half in range(2):
-                    at = base + QUAD + 4 * leaf + 2 * coord + half
-                    ref[at : at + 1, :] = place[
-                        coord : coord + 1, half * HALF : (half + 1) * HALF
-                    ]
+        message[leaf * RANK : (leaf + 1) * RANK, :] = coef
         part = mm3(transfer[leaf], coef, (0, 0))
         total = part if leaf == 0 else total + part
-
-        @pl.when(parity == row)
-        def _():
-            (a_right if col else a_left)[:PTS, :] = values
-            to_y[col * PTS : (col + 1) * PTS, :] = values
-
-        @pl.when(parity != row)
-        def _():
-            (b_right if col else b_left)[...] = values
-            to_c[col * PTS : (col + 1) * PTS, :] = values
-
     dev[...] = total
+    for target in (
+        a_right.at[PTS:], a_left.at[PTS:], to_y.at[2 * PTS :], to_c.at[2 * PTS :]
+    ):
+        copy = pltpu.make_async_copy(message, target, sems.at[len(copies)])
+        copy.start()
+        copies.append(copy)
+    for copy in copies:
+        copy.wait()
 
 
 def coefficients(losses, basis, transfer, positions):
+    hbm = pl.BlockSpec(memory_space=pl.ANY)
     return pl.pallas_call(
         coef_kernel,
-        in_specs=[whole] * 4,
-        out_specs=[whole] * 8,
+        in_specs=[hbm, hbm, whole, whole],
+        out_specs=[hbm] * 6 + [whole] * 2,
         out_shape=[
             shape(PTS + MSG, COLS),
             shape(PTS + MSG, COLS),
@@ -109,10 +134,15 @@
             shape(4, PTS, 8),
             shape(RANK, COLS),
         ],
-        compiler_params=params(16),
-        cost_estimate=pl.CostEstimate(
-            flops=1_000_000_000, bytes_accessed=6_000_000, transcendentals=0
-        ),
+        scratch_shapes=[
+            VMEM((4, PTS, COLS), f32),
+            VMEM((4, RANK, PTS), f32),
+            VMEM((MSG, COLS), f32),
+            pltpu.SemaphoreType.DMA((12,)),
+            pltpu.SemaphoreType.DMA((8,)),
+        ],
+        compiler_params=params(),
+        cost_estimate=COST,
         name="coefs",
     )(losses, basis, transfer, positions)
 
@@ -191,12 +221,7 @@
             step(2 * pair + 1, kern_b, kern_a)
 
 
-def near_cost(n_pairs):
-    return pl.CostEstimate(
-        flops=n_pairs * 500_000_000,
-        bytes_accessed=4_000_000,
-        transcendentals=n_pairs * 2 * PTS * PTS,
-    )
+COST = pl.CostEstimate(flops=20_000_000_000, bytes_accessed=4_000_000, transcendentals=0)
 
 
 ACC = shape(4, PTS, COLS)
@@ -210,19 +235,19 @@
     near_blocks(flags, tpos, slots, pairs, acc, scratch)
 
 
-def lat_kernel(flags, tpos, from_y, from_c, before, acc, *scratch):
+def lat_kernel(is_c, flags, tpos, source, before, acc, *scratch):
     acc[...] = before[...]
     parity = lat_parity()
     base = 2 * PTS + QUAD
-    slots, pairs = [], []
-    for ref, place, row, own_row in (
-        (from_y, 8 - 8 * parity, 3 * parity - 1, parity),
-        (from_c, 8 * parity, 2 - 3 * parity, 1 - parity),
-    ):
-        for col in range(2):
-            for own_col in range(2):
-                pairs.append((len(slots), row, col, own_row, own_col))
-            slots.append((ref[col * PTS : (col + 1) * PTS, :], ref, base + place + 4 * col))
+    if is_c:
+        place, row, own_row = 8 * parity, 2 - 3 * parity, 1 - parity
+    else:
+        place, row, own_row = 8 - 8 * parity, 3 * parity - 1, parity
+    slots = [
+        (source[col * PTS : (col + 1) * PTS, :], source, base + place + 4 * col)
+        for col in range(2)
+    ]
+    pairs = [(col, row, col, own_row, own_col) for col in range(2) for own_col in range(2)]
     near_blocks(flags, tpos, slots, pairs, acc, scratch)
 
 
@@ -239,19 +264,21 @@
     near_blocks(flags, tpos, slots, pairs, acc, scratch)
 
 
-def last_kernel(flags, tpos, a_left, a_right, left, right, c_ends, left_c, right_c, before, acc, *scratch):
+def last_kernel(flags, tpos, a_left, a_right, left, right, before, acc, *scratch):
     acc[...] = before[...]
     parity = lat_parity()
     base = PTS + QUAD + 8 - 8 * parity
+    slots = [(left[...], a_left, base + 4), (right[...], a_right, base)]
+    pairs = [(s, 1 - parity, 3 * s - 1, i, s) for s in range(2) for i in range(2)]
+    near_blocks(flags, tpos, slots, pairs, acc, scratch)
+
+
+def corner_kernel(flags, tpos, c_ends, left_c, right_c, before, acc, *scratch):
+    acc[...] = before[...]
+    parity = lat_parity()
     ends = 2 * QUAD + 8 * parity
-    slots = [
-        (left[...], a_left, base + 4),
-        (right[...], a_right, base),
-        (left_c[...], c_ends, ends + 4),
-        (right_c[...], c_ends, ends + 16),
-    ]
-    pairs = [(s, 1 - parity, 3 * s - 1, i, s) for s in range(2) for i in range(2)]
-    pairs += [(2 + s, 2 - 3 * parity, 3 * s - 1, 1 - parity, s) for s in range(2)]
+    slots = [(left_c[...], c_ends, ends + 4), (right_c[...], c_ends, ends + 16)]
+    pairs = [(s, 2 - 3 * parity, 3 * s - 1, 1 - parity, s) for s in range(2)]
     near_blocks(flags, tpos, slots, pairs, acc, scratch)
 
 
@@ -264,7 +291,7 @@
         scratch_shapes=near_scratch(n_slots, n_pairs),
         input_output_aliases={len(operands) - 1: 0} if chained else {},
         compiler_params=params(),
-        cost_estimate=near_cost(n_pairs),
+        cost_estimate=COST,
         name=name,
     )(*operands)
 
@@ -355,9 +382,7 @@
         out_shape=shape(QUAD, COLS),
         scratch_shapes=[VMEM((n_lat // 2, n_lon // 2, RANK, RANK), bf16)],
         compiler_params=params(),
-        cost_estimate=pl.CostEstimate(
-            flops=6_000_000_000, bytes_accessed=9_000_000, transcendentals=0
-        ),
+        cost_estimate=COST,
         name="far",
     )(*operands)
 
@@ -414,26 +439,29 @@
     )
     left = lax.ppermute(a_right, "lon", to_right)
     right = lax.ppermute(a_left, "lon", to_left)
-    from_c = lax.ppermute(to_c, "lat", in_chip)
     left_b = lax.ppermute(b_right, "lon", to_right)
     right_b = lax.ppermute(b_left, "lon", to_left)
     from_y = lax.ppermute(to_y, "lat", across)
 
-    pairs = [[2 * k, 2 * k + 1] for k in range(n_lon // 2)]
-    classes = [list(range(j, n_lon, 2)) for j in range(2)]
-    every = lax.all_gather(dev, "lon", axis_index_groups=pairs)
-    every = lax.all_gather(every, "lon", axis_index_groups=classes)
-    every = lax.all_gather(every, "lat")
-    every = every.reshape(n_lat * n_lon, RANK, COLS)
+    every = lax.all_gather(dev, "lon")
 
     (acc,) = near(own_kernel, "own", 4, 16, (flags, tpos, flat, a_right), chained=False)
-    (acc,) = near(lat_kernel, "lat", 4, 8, (flags, tpos, from_y, from_c, acc))
+    to_c, from_y, every, acc = lax.optimization_barrier((to_c, from_y, every, acc))
+    from_c = lax.ppermute(to_c, "lat", in_chip)
+    every = lax.all_gather(every, "lat").reshape(n_lat * n_lon, RANK, COLS)
+    (acc,) = near(
+        functools.partial(lat_kernel, False), "lat_y", 2, 4, (flags, tpos, from_y, acc)
+    )
+    (acc,) = near(
+        functools.partial(lat_kernel, True), "lat_c", 2, 4, (flags, tpos, from_c, acc)
+    )
     left, right, acc = lax.optimization_barrier((left, right, acc))
     left_y = lax.ppermute(left, "lat", across)
     right_y = lax.ppermute(right, "lat", across)
     acc, to_c = near(
         lon_kernel, "lon", 2, 4, (flags, tpos, left, right, acc), more=[shape(2 * MSG, COLS)]
     )
+    every, acc = lax.optimization_barrier((every, acc))
     c_ends = lax.ppermute(to_c, "lat", in_chip)
     partial = far_field(
         n_lat,
@@ -453,8 +481,7 @@
             transfer,
         ),
     )
-    left_c = lax.ppermute(left_b, "lat", in_chip)
-    right_c = lax.ppermute(right_b, "lat", in_chip)
+    left_y, right_y, partial = lax.optimization_barrier((left_y, right_y, partial))
     (acc,) = near(
         down_kernel,
         "down",
@@ -462,12 +489,15 @@
         2,
         (flags, tpos, weights, left_y, right_y, c_ends, partial, basis, acc),
     )
+    left_b, right_b, acc = lax.optimization_barrier((left_b, right_b, acc))
+    left_c = lax.ppermute(left_b, "lat", in_chip)
+    right_c = lax.ppermute(right_b, "lat", in_chip)
     (acc,) = near(
-        last_kernel,
-        "last",
-        4,
-        6,
-        (flags, tpos, left, right, left_b, right_b, c_ends, left_c, right_c, acc),
+        last_kernel, "last", 2, 4, (flags, tpos, left, right, left_b, right_b, acc)
+    )
+    left_c, right_c, acc = lax.optimization_barrier((left_c, right_c, acc))
+    (acc,) = near(
+        corner_kernel, "corner", 2, 2, (flags, tpos, c_ends, left_c, right_c, acc)
     )
     return acc.reshape(2, 2, PTS, COLS)
 

time: 149 us -> 311 us (2.09); the launches traced: 147 us -> 306 us
  Pallas kernels: 41.7 us -> 189 us
  blocking collectives: 16.7 us -> 75.8 us
  waiting for transfers between devices: 36.4 us -> 5.59 us
  local copies, waits for them, and re-layouts: 19.8 us -> 0 us
    pallas_call x1, Pallas kernels: 1.87 us -> 130 us  [coefficients(): pl.pallas_call(coef_kernel, in_specs=[hbm, hbm, whole, whole], out_specs=...]
    all_gather x2 -> x1, blocking collectives: 16.7 us -> 75.8 us  [local(): every = lax.all_gather(dev, 'lon')]
    ppermute x1, waiting for transfers between devices: 24.5 us -> 0.01 us  [local(): from_y = lax.ppermute(to_y, 'lat', across)]
    unnamed x50 -> x0, local copies, waits for them, and re-layouts: 19.8 us -> none
    pallas_call x5 -> x7, Pallas kernels: 35.3 us -> 50.4 us  [near(): pl.pallas_call(kernel, in_specs=[scalars] + [whole] * (len(operands) - 1)...]
    ppermute x1, waiting for transfers between devices: 0.01 us -> 5.53 us  [local(): right_y = lax.ppermute(right, 'lat', across)]
    ppermute x1, starting transfers between devices: 0.07 us -> 4.99 us  [local(): from_c = lax.ppermute(to_c, 'lat', in_chip)]
    ppermute x1, waiting for transfers between devices: 4.85 us -> 0.01 us  [local(): left = lax.ppermute(a_right, 'lon', to_right)]
  transfers between devices with their start and end apart: 12 -> 12, of which waited for: 5 -> 1; matrix products, arithmetic and copies ran while one was open for 0% -> 0% of each run, Pallas kernels for 23% -> 18%
where the time goes in v1:
time: 311 us; the launch traced here: 306 us
  Pallas kernels  189 us (61%)
  blocking collectives  75.8 us (24%)
  starting transfers between devices  21.7 us (7%)
  between operations  13.4 us (4%)
  waiting for transfers between devices  5.59 us (2%)
    pallas_call x1, Pallas kernels, coefficients(): pl.pallas_call(coef_kernel, in_specs=[hbm, hbm, whole, whole], out_specs=...  130 us
    all_gather x1, blocking collectives, local(): every = lax.all_gather(dev, 'lon')  75.8 us
    pallas_call x7, Pallas kernels, near(): pl.pallas_call(kernel, in_specs=[scalars] + [whole] * (len(operands) - 1)...  50.4 us
    pallas_call x1, Pallas kernels, far_field(): pl.pallas_call(functools.partial(far_kernel, n_lat, n_lon), in_specs=spec...  8.73 us
  transfers between devices with their start and end apart: 12, of which 1 were waited for; matrix products, arithmetic and copies ran while one was open for 0% of the time, Pallas kernels for 18%

profile of v1, /device:TPU:9, one launch (start us, length us, event | category | flops | bytes accessed | tf_op | source)
XLA Modules:
  0.0 306.0 jit_solution(8962162956786253810)
XLA Ops:
  6.5 130.3 %coefs.1 = (f32[784,256]{1,0:T(8,128)}, f32[784,256]{1,0:T(8,128)}, f32[512,256]{1,0:T(8,128)}, f32[512,256]{1,0:T(8,128)}, f32[1296,256]{1,0:T(8,128)}, /*index...) custom-call(f32[4,512,256]{2,1,0:T(8,128)} %bitcast.15, f32[4,64,512]{2,1,0:T(8,128)} %bitcast.19, ...), custom_call_target="tpu_custom_call" | custom-call | flops 20000000000 | bytes 4000000 | tf_op jit(solution)/shard_map/coefs/pallas_call | solution.py:123
  136.8 3.7 %collective-permute-start.2 = (f32[1296,256]{1,0:T(8,128)}, f32[1296,256]{1,0:T(8,128)}, u32[]{:S(2)}, u32[]{:S(2)}) collective-permute-start(f32[1296,256]{1,0:T(8,128)} %get-tuple-element.37), channel_id=1, source_target_pairs={{8,16},{16,8},{9,17},{17,9},{10,18},{18,10},{11,19},{19,11},{12,20... | collective-permute-start | bytes 3981320 | tf_op jit(solution)/shard_map/ppermute | solution.py:444
  140.5 1.3 collective-permute-start
  141.8 1.2 collective-permute-start.1
  142.9 0.3 collective-permute-start.5
  143.3 2.1 collective-permute-start.6
  145.3 75.8 %all-gather = f32[512,256]{1,0:T(8,128)} all-gather(f32[64,256]{1,0:T(8,128)} %get-tuple-element.38), channel_id=2, replica_groups=mesh['lat'=4,'lon'=8] {'lon'}, dimensions={0}, use_global_device_ids=true | all-gather | bytes 589824 | tf_op jit(solution)/shard_map/all_gather | solution.py:446
  221.1 13.3 %own.1.before = f32[4,512,256]{2,1,0:T(8,128)} custom-call(s32[4,9]{1,0:T(4,128)} %bitcast.24, f32[4,512,8]{2,1,0:T(8,128)} %get-tuple-element.33.tpos, f32[4,512,256]{2,1,0:T(8,128)} %bitcast.16, f32[784,256]{1,0:T(8,128)} %get-tuple-element.34.msg.own), custom_call_target="tpu_custom_call" | custom-call | flops 20000000000 | bytes 4000000 | tf_op jit(solution)/shard_map/own/pallas_call | solution.py:286
  234.4 0.0 collective-permute-done.2.source.from_y
  234.4 5.0 %collective-permute-start.3 = (f32[1296,256]{1,0:T(8,128)}, f32[1296,256]{1,0:T(8,128)}, u32[]{:S(2)}, u32[]{:S(2)}) collective-permute-start(f32[1296,256]{1,0:T(8,128)} %get-tuple-element.39), channel_id=1, source_target_pairs={{0,8},{8,0},{16,24},{24,16},{1,9},{9,1},{17,25},{25,17},{2,10},{10... | collective-permute-start | bytes 3981320 | tf_op jit(solution)/shard_map/ppermute | solution.py:450
  239.4 0.0 all-gather.4.cloned.1.call-update
  239.5 6.4 %lat_y.1.before = f32[4,512,256]{2,1,0:T(8,128)} custom-call(s32[4,9]{1,0:T(4,128)} %bitcast.25, f32[4,512,8]{2,1,0:T(8,128)} %get-tuple-element.33.tpos, f32[1296,256]{1,0:T(8,128)} %collective-permute-done.2.source.from_y, f32[4,512,256]{2,1,0:T(8,128)} %own.1.before), custom_call_target="tpu_custom_call", output_to_operand_aliasing={{}: (3, {})} | custom-call | flops 20000000000 | bytes 4000000 | tf_op jit(solution)/shard_map/lat_y/pallas_call | solution.py:286
  245.8 0.0 collective-permute-done.3.source.from_c
  245.8 7.3 %lat_c.1.before = f32[4,512,256]{2,1,0:T(8,128)} custom-call(s32[4,9]{1,0:T(4,128)} %bitcast.26, f32[4,512,8]{2,1,0:T(8,128)} %get-tuple-element.33.tpos, f32[1296,256]{1,0:T(8,128)} %collective-permute-done.3.source.from_c, f32[4,512,256]{2,1,0:T(8,128)} %lat_y.1.before), custom_call_target="tpu_custom_call", output_to_operand_aliasing={{}: (3, {})} | custom-call | flops 20000000000 | bytes 4000000 | tf_op jit(solution)/shard_map/lat_c/pallas_call | solution.py:286
  253.1 0.0 collective-permute-done.left.a_left
  253.1 0.0 collective-permute-done.1.right.a_right
  253.1 5.8 %collective-permute-start.7 = (f32[784,256]{1,0:T(8,128)}, f32[784,256]{1,0:T(8,128)}, u32[]{:S(2)}, u32[]{:S(2)}) collective-permute-start(f32[784,256]{1,0:T(8,128)} %collective-permute-done.left.a_left), channel_id=1, source_target_pairs={{8,16},{16,8},{9,17},{17,9},{10,18},{18,10},{11,19},{19,11},{12,20... | collective-permute-start | bytes 2408456 | tf_op jit(solution)/shard_map/ppermute | solution.py:459
  258.9 1.9 collective-permute-start.8
  260.8 4.5 %lon.1 = (f32[4,512,256]{2,1,0:T(8,128)}, f32[544,256]{1,0:T(8,128)}) custom-call(s32[4,9]{1,0:T(4,128)} %bitcast.27, f32[4,512,8]{2,1,0:T(8,128)} %get-tuple-element.33.tpos, f32[784,256]{1,0:T(8,128)} %collective-permute-done.left.a_left, f32[784,256]{1,0:T(8,128)} %collective-permute-done.1.right.a_right, ...), custom_call_target="tpu_custom_call", output_to_operand_aliasing={{0}: (4, {})} | custom-call | flops 20000000000 | bytes 4000000 | tf_op jit(solution)/shard_map/lon/pallas_call | solution.py:286
  265.3 0.0 collective-permute-start.4
  265.3 0.0 all-gather.4.cloned.1.call-done.every
  265.3 8.7 %far.1.partial = f32[256,256]{1,0:T(8,128)} custom-call(s32[4,9]{1,0:T(4,128)} %bitcast.28, bf16[4,36,64,64]{3,2,1,0:T(8,128)(2,1)} %bitcast.13, f32[784,256]{1,0:T(8,128)} %get-tuple-element.34.msg.own, f32[784,256]{1,0:T(8,128)} %collective-permute-done.left.a_left, f32[784,256]{1,0:T(8,128)} %collective-permute-done.1.right.a_right, ...), custom_call_target="tpu_custom_call" | custom-call | flops 20000000000 | bytes 4000000 | tf_op jit(solution)/shard_map/far/pallas_call | solution.py:378
  274.1 0.0 collective-permute-done.7.left_y
  274.1 5.5 %collective-permute-done.8.right_y = f32[784,256]{1,0:T(8,128)} collective-permute-done((f32[784,256]{1,0:T(8,128)}, f32[784,256]{1,0:T(8,128)}, u32[]{:S(2)}, u32[]{:S(2)}) %collective-permute-start.8) | collective-permute-done | bytes 802848 | tf_op jit(solution)/shard_map/ppermute | solution.py:460
  279.6 0.0 collective-permute-done.4.c_ends
  279.6 8.8 %down.1.before = f32[4,512,256]{2,1,0:T(8,128)} custom-call(s32[4,9]{1,0:T(4,128)} %bitcast.29, f32[4,512,8]{2,1,0:T(8,128)} %get-tuple-element.33.tpos, bf16[4,36,64,64]{3,2,1,0:T(8,128)(2,1)} %bitcast.14, f32[784,256]{1,0:T(8,128)} %collective-permute-done.7.left_y, f32[784,256]{1,0:T(8,128)} %collective-permute-done.8.right_y, ...), custom_call_target="tpu_custom_call", output_to_operand_aliasing={{}: (8, {})} | custom-call | flops 20000000000 | bytes 4000000 | tf_op jit(solution)/shard_map/down/pallas_call | solution.py:286
  288.4 0.1 collective-permute-start.10
  288.5 0.5 collective-permute-start.9
  289.0 5.9 %last.1.before = f32[4,512,256]{2,1,0:T(8,128)} custom-call(s32[4,9]{1,0:T(4,128)} %bitcast.30, f32[4,512,8]{2,1,0:T(8,128)} %get-tuple-element.33.tpos, f32[784,256]{1,0:T(8,128)} %collective-permute-done.left.a_left, f32[784,256]{1,0:T(8,128)} %collective-permute-done.1.right.a_right, ...), custom_call_target="tpu_custom_call", output_to_operand_aliasing={{}: (6, {})} | custom-call | flops 20000000000 | bytes 4000000 | tf_op jit(solution)/shard_map/last/pallas_call | solution.py:286
  294.9 0.0 collective-permute-done.10.right_c
  294.9 0.0 collective-permute-done.9.left_c
  294.9 4.3 %corner.1 = f32[4,512,256]{2,1,0:T(8,128)} custom-call(s32[4,9]{1,0:T(4,128)} %bitcast.31, f32[4,512,8]{2,1,0:T(8,128)} %get-tuple-element.33.tpos, f32[544,256]{1,0:T(8,128)} %collective-permute-done.4.c_ends, f32[512,256]{1,0:T(8,128)} %collective-permute-done.9.left_c, ...), custom_call_target="tpu_custom_call", output_to_operand_aliasing={{}: (5, {})} | custom-call | flops 20000000000 | bytes 4000000 | tf_op jit(solution)/shard_map/corner/pallas_call | solution.py:286
  (3 shorter events, 0.0 us)
Async XLA Ops:
  6.5 258.8 %all-gather.4.cloned.1.call-start = ((), (), s32[]{:S(2)}) async-start(), calls=%async_computation | async-start | bytes 2621440 | tf_op jit(solution)/shard_map/all_gather | solution.py:451
  136.8 97.6 %collective-permute-start.2 = (f32[1296,256]{1,0:T(8,128)}, f32[1296,256]{1,0:T(8,128)}, u32[]{:S(2)}, u32[]{:S(2)}) collective-permute-start(f32[1296,256]{1,0:T(8,128)} %get-tuple-element.37), channel_id=1, source_target_pairs={{8,16},{16,8},{9,17},{17,9},{10,18},{18,10},{11,19},{19,11},{12,20... | collective-permute-start | bytes 3981320 | tf_op jit(solution)/shard_map/ppermute | solution.py:444
  140.5 112.6 %collective-permute-start = (f32[784,256]{1,0:T(8,128)}, f32[784,256]{1,0:T(8,128)}, u32[]{:S(2)}, u32[]{:S(2)}) collective-permute-start(f32[784,256]{1,0:T(8,128)} %get-tuple-element.34.msg.own), channel_id=1, source_target_pairs={{0,1},{1,2},{2,3},{3,4},{4,5},{5,6},{6,7},{7,0},{8,9},{9,10},{10,1... | collective-permute-start | bytes 2408456 | tf_op jit(solution)/shard_map/ppermute | solution.py:440
  141.8 111.4 %collective-permute-start.1 = (f32[784,256]{1,0:T(8,128)}, f32[784,256]{1,0:T(8,128)}, u32[]{:S(2)}, u32[]{:S(2)}) collective-permute-start(f32[784,256]{1,0:T(8,128)} %get-tuple-element.35), channel_id=1, source_target_pairs={{0,7},{1,0},{2,1},{3,2},{4,3},{5,4},{6,5},{7,6},{8,15},{9,8},{10,9... | collective-permute-start | bytes 2408456 | tf_op jit(solution)/shard_map/ppermute | solution.py:441
  142.9 145.4 %collective-permute-start.5 = (f32[512,256]{1,0:T(8,128)}, f32[512,256]{1,0:T(8,128)}, u32[]{:S(2)}, u32[]{:S(2)}) collective-permute-start(f32[512,256]{1,0:T(8,128)} %get-tuple-element.46), channel_id=1, source_target_pairs={{0,1},{1,2},{2,3},{3,4},{4,5},{5,6},{6,7},{7,0},{8,9},{9,10},{10,1... | collective-permute-start | bytes 1572872 | tf_op jit(solution)/shard_map/ppermute | solution.py:442
  143.3 145.1 %collective-permute-start.6 = (f32[512,256]{1,0:T(8,128)}, f32[512,256]{1,0:T(8,128)}, u32[]{:S(2)}, u32[]{:S(2)}) collective-permute-start(f32[512,256]{1,0:T(8,128)} %get-tuple-element.47), channel_id=1, source_target_pairs={{0,7},{1,0},{2,1},{3,2},{4,3},{5,4},{6,5},{7,6},{8,15},{9,8},{10,9... | collective-permute-start | bytes 1572872 | tf_op jit(solution)/shard_map/ppermute | solution.py:443
  234.4 11.4 %collective-permute-start.3 = (f32[1296,256]{1,0:T(8,128)}, f32[1296,256]{1,0:T(8,128)}, u32[]{:S(2)}, u32[]{:S(2)}) collective-permute-start(f32[1296,256]{1,0:T(8,128)} %get-tuple-element.39), channel_id=1, source_target_pairs={{0,8},{8,0},{16,24},{24,16},{1,9},{9,1},{17,25},{25,17},{2,10},{10... | collective-permute-start | bytes 3981320 | tf_op jit(solution)/shard_map/ppermute | solution.py:450
  253.1 20.9 %collective-permute-start.7 = (f32[784,256]{1,0:T(8,128)}, f32[784,256]{1,0:T(8,128)}, u32[]{:S(2)}, u32[]{:S(2)}) collective-permute-start(f32[784,256]{1,0:T(8,128)} %collective-permute-done.left.a_left), channel_id=1, source_target_pairs={{8,16},{16,8},{9,17},{17,9},{10,18},{18,10},{11,19},{19,11},{12,20... | collective-permute-start | bytes 2408456 | tf_op jit(solution)/shard_map/ppermute | solution.py:459
  258.9 20.7 %collective-permute-start.8 = (f32[784,256]{1,0:T(8,128)}, f32[784,256]{1,0:T(8,128)}, u32[]{:S(2)}, u32[]{:S(2)}) collective-permute-start(f32[784,256]{1,0:T(8,128)} %collective-permute-done.1.right.a_right), channel_id=1, source_target_pairs={{8,16},{16,8},{9,17},{17,9},{10,18},{18,10},{11,19},{19,11},{12,20... | collective-permute-start | bytes 2408456 | tf_op jit(solution)/shard_map/ppermute | solution.py:460
  265.3 14.3 %collective-permute-start.4 = (f32[544,256]{1,0:T(8,128)}, f32[544,256]{1,0:T(8,128)}, u32[]{:S(2)}, u32[]{:S(2)}) collective-permute-start(f32[544,256]{1,0:T(8,128)} %get-tuple-element.45), channel_id=1, source_target_pairs={{0,8},{8,0},{16,24},{24,16},{1,9},{9,1},{17,25},{25,17},{2,10},{10... | collective-permute-start | bytes 1671176 | tf_op jit(solution)/shard_map/ppermute | solution.py:465
  288.4 6.5 %collective-permute-start.10 = (f32[512,256]{1,0:T(8,128)}, f32[512,256]{1,0:T(8,128)}, u32[]{:S(2)}, u32[]{:S(2)}) collective-permute-start(f32[512,256]{1,0:T(8,128)} %collective-permute-done.6.right), channel_id=1, source_target_pairs={{0,8},{8,0},{16,24},{24,16},{1,9},{9,1},{17,25},{25,17},{2,10},{10... | collective-permute-start | bytes 1572872 | tf_op jit(solution)/shard_map/ppermute | solution.py:494
  288.5 6.4 %collective-permute-start.9 = (f32[512,256]{1,0:T(8,128)}, f32[512,256]{1,0:T(8,128)}, u32[]{:S(2)}, u32[]{:S(2)}) collective-permute-start(f32[512,256]{1,0:T(8,128)} %collective-permute-done.5.left), channel_id=1, source_target_pairs={{0,8},{8,0},{16,24},{24,16},{1,9},{9,1},{17,25},{25,17},{2,10},{10... | collective-permute-start | bytes 1572872 | tf_op jit(solution)/shard_map/ppermute | solution.py:493
Sparse Core Ops, SparseCore 0:
  239.6 25.7 all-gather.3

commit v2 on v1

--- a/solution.py
+++ b/solution.py
@@ -51,6 +51,10 @@
     return pltpu.CompilerParams(vmem_limit_bytes=limit * 1024 * 1024)
 
 
+COST = pl.CostEstimate(flops=20_000_000_000, bytes_accessed=4_000_000, transcendentals=0)
+LOW = pl.CostEstimate(flops=1_000, bytes_accessed=1_000, transcendentals=0)
+
+
 def shape(*dims):
     return jax.ShapeDtypeStruct(dims, f32)
 
@@ -60,20 +64,30 @@
 
 
 def coef_kernel(
-    loss, basis, transfer, pos, a_right, a_left, b_right, b_left, to_y, to_c, tpos, dev,
+    loss, basis, transfer, pos, a_right, a_left, b_right, b_left, to_y, to_c, place8, dev,
     values, bases, message, sems, load_sems,
 ):
     parity = lat_parity()
-    loads = []
+    loads = [
+        (
+            pltpu.make_async_copy(loss.at[leaf], values.at[leaf], load_sems.at[leaf]),
+            pltpu.make_async_copy(basis.at[leaf], bases.at[leaf], load_sems.at[4 + leaf]),
+        )
+        for leaf in range(4)
+    ]
+    for pair in loads:
+        for copy in pair:
+            copy.start()
     for leaf in range(4):
-        loads.append(
-            (
-                pltpu.make_async_copy(loss.at[leaf], values.at[leaf], load_sems.at[leaf]),
-                pltpu.make_async_copy(basis.at[leaf], bases.at[leaf], load_sems.at[4 + leaf]),
-            )
-        )
-        for copy in loads[-1]:
-            copy.start()
+        place = pos[leaf] * UNIT
+        place8[leaf] = jnp.concatenate([place, jnp.zeros((6, PTS), f32)], 0)
+        for coord in range(2):
+            for half in range(2):
+                at = QUAD + 4 * leaf + 2 * coord + half
+                message[at : at + 1, :] = place[coord : coord + 1, half * HALF : (half + 1) * HALF]
+    for pair in loads:
+        for copy in pair:
+            copy.wait()
     y_row, c_row = 2 * parity, 2 - 2 * parity
     first, second = slice(0, PTS), slice(PTS, 2 * PTS)
     copies = []
@@ -87,20 +101,11 @@
         (c_row, to_c.at[first]),
         (c_row + 1, to_c.at[second]),
     ):
-        copy = pltpu.make_async_copy(loss.at[source], target, sems.at[len(copies)])
+        copy = pltpu.make_async_copy(values.at[source], target, sems.at[len(copies)])
         copy.start()
         copies.append(copy)
-    for leaf in range(4):
-        place = pos[leaf] * UNIT
-        tpos[leaf] = jnp.concatenate([place, jnp.zeros((6, PTS), f32)], 0).T
-        for coord in range(2):
-            for half in range(2):
-                at = QUAD + 4 * leaf + 2 * coord + half
-                message[at : at + 1, :] = place[coord : coord + 1, half * HALF : (half + 1) * HALF]
     total = None
     for leaf in range(4):
-        for copy in loads[leaf]:
-            copy.wait()
         l_hi, l_lo = split(values[leaf])
         b_hi, b_lo = split(bases[leaf])
         coef = mm(b_hi, l_hi) + (mm(b_lo, l_hi) + mm(b_hi, l_lo))
@@ -118,8 +123,10 @@
         copy.wait()
 
 
+hbm = pl.BlockSpec(memory_space=pl.ANY)
+
+
 def coefficients(losses, basis, transfer, positions):
-    hbm = pl.BlockSpec(memory_space=pl.ANY)
     return pl.pallas_call(
         coef_kernel,
         in_specs=[hbm, hbm, whole, whole],
@@ -131,7 +138,7 @@
             shape(PTS, COLS),
             shape(2 * PTS + MSG, COLS),
             shape(2 * PTS + MSG, COLS),
-            shape(4, PTS, 8),
+            shape(4, 8, PTS),
             shape(RANK, COLS),
         ],
         scratch_shapes=[
@@ -150,15 +157,28 @@
 def near_scratch(n_slots, n_pairs):
     return [
         SMEM((n_pairs + 1, 8), jnp.int32),
+        VMEM((4, PTS, 8), f32),
         VMEM((n_slots, 8, PTS), f32),
         VMEM((n_slots, 2 * PTS, COLS), bf16),
         VMEM((PTS, 2 * PTS), bf16),
         VMEM((PTS, 2 * PTS), bf16),
+        VMEM((4, PTS, COLS), f32),
+        pltpu.SemaphoreType.DMA((8,)),
     ]
 
 
-def near_blocks(flags, tpos, slots, pairs, acc, scratch):
-    table, spos, stack, kern_a, kern_b = scratch
+def near_blocks(flags, place8, slots, pairs, before, out, scratch, fill=None):
+    table, tpos, spos, stack, kern_a, kern_b, acc, sems = scratch
+    loads = []
+    if before is not None:
+        loads = [
+            pltpu.make_async_copy(before.at[leaf], acc.at[leaf], sems.at[leaf])
+            for leaf in range(4)
+        ]
+    for copy in loads:
+        copy.start()
+    for leaf in range(4):
+        tpos[leaf] = place8[leaf].T
     for slot, (values, places, base) in enumerate(slots):
         hi, lo = split(values)
         stack[slot, :PTS, :] = hi
@@ -212,6 +232,11 @@
         for half in range(2):
             evaluate(0, half, kern_a)
 
+    for copy in loads:
+        copy.wait()
+    if fill is not None:
+        fill(acc)
+
     @pl.loop(0, (count + 1) // 2)
     def _(pair):
         step(2 * pair, kern_a, kern_b)
@@ -221,77 +246,79 @@
             step(2 * pair + 1, kern_b, kern_a)
 
 
-COST = pl.CostEstimate(flops=20_000_000_000, bytes_accessed=4_000_000, transcendentals=0)
+    stores = [
+        pltpu.make_async_copy(acc.at[leaf], out.at[leaf], sems.at[4 + leaf]) for leaf in range(4)
+    ]
+    for copy in stores:
+        copy.start()
+    for copy in stores:
+        copy.wait()
 
 
 ACC = shape(4, PTS, COLS)
 
 
-def own_kernel(flags, tpos, loss, msg, acc, *scratch):
+def own_kernel(flags, place8, loss, msg, out, *scratch):
     slots = [(loss[leaf], msg, PTS + QUAD + 4 * leaf) for leaf in range(4)]
     pairs = [(s, s // 2, s % 2, t // 2, t % 2) for s in range(4) for t in range(4)]
-    for leaf in range(4):
-        acc[leaf] = 0.5 * loss[leaf]
-    near_blocks(flags, tpos, slots, pairs, acc, scratch)
-
-
-def lat_kernel(is_c, flags, tpos, source, before, acc, *scratch):
-    acc[...] = before[...]
+
+    def fill(acc):
+        for leaf in range(4):
+            acc[leaf] = 0.5 * loss[leaf]
+
+    near_blocks(flags, place8, slots, pairs, None, out, scratch, fill)
+
+
+def lat_kernel(flags, place8, from_y, from_c, before, out, *scratch):
     parity = lat_parity()
     base = 2 * PTS + QUAD
-    if is_c:
-        place, row, own_row = 8 * parity, 2 - 3 * parity, 1 - parity
-    else:
-        place, row, own_row = 8 - 8 * parity, 3 * parity - 1, parity
-    slots = [
-        (source[col * PTS : (col + 1) * PTS, :], source, base + place + 4 * col)
-        for col in range(2)
-    ]
-    pairs = [(col, row, col, own_row, own_col) for col in range(2) for own_col in range(2)]
-    near_blocks(flags, tpos, slots, pairs, acc, scratch)
-
-
-def lon_kernel(flags, tpos, left, right, before, acc, to_c, *scratch):
-    acc[...] = before[...]
+    slots, pairs = [], []
+    for ref, place, row, own_row in (
+        (from_y, 8 - 8 * parity, 3 * parity - 1, parity),
+        (from_c, 8 * parity, 2 - 3 * parity, 1 - parity),
+    ):
+        for col in range(2):
+            for own_col in range(2):
+                pairs.append((len(slots), row, col, own_row, own_col))
+            slots.append((ref[col * PTS : (col + 1) * PTS, :], ref, base + place + 4 * col))
+    near_blocks(flags, place8, slots, pairs, before, out, scratch)
+
+
+def lon_kernel(flags, place8, left, right, before, out, *scratch):
     parity = lat_parity()
-    to_c[:QUAD, :] = left[PTS : PTS + QUAD, :]
-    to_c[QUAD : 2 * QUAD, :] = right[PTS : PTS + QUAD, :]
-    to_c[2 * QUAD : 2 * QUAD + 16, :] = left[PTS + QUAD :, :]
-    to_c[2 * QUAD + 16 :, :] = right[PTS + QUAD :, :]
     base = PTS + QUAD + 8 * parity
     slots = [(left[:PTS, :], left, base + 4), (right[:PTS, :], right, base)]
     pairs = [(s, parity, 3 * s - 1, i, s) for s in range(2) for i in range(2)]
-    near_blocks(flags, tpos, slots, pairs, acc, scratch)
-
-
-def last_kernel(flags, tpos, a_left, a_right, left, right, before, acc, *scratch):
-    acc[...] = before[...]
+    near_blocks(flags, place8, slots, pairs, before, out, scratch)
+
+
+def last_kernel(
+    flags, place8, a_left, a_right, left, right, c_ends, left_c, right_c, before, out, *scratch
+):
     parity = lat_parity()
     base = PTS + QUAD + 8 - 8 * parity
-    slots = [(left[...], a_left, base + 4), (right[...], a_right, base)]
+    ends = QUAD + 8 * parity
+    slots = [
+        (left[...], a_left, base + 4),
+        (right[...], a_right, base),
+        (left_c[...], c_ends, ends + 4),
+        (right_c[...], c_ends, MSG + ends),
+    ]
     pairs = [(s, 1 - parity, 3 * s - 1, i, s) for s in range(2) for i in range(2)]
-    near_blocks(flags, tpos, slots, pairs, acc, scratch)
-
-
-def corner_kernel(flags, tpos, c_ends, left_c, right_c, before, acc, *scratch):
-    acc[...] = before[...]
-    parity = lat_parity()
-    ends = 2 * QUAD + 8 * parity
-    slots = [(left_c[...], c_ends, ends + 4), (right_c[...], c_ends, ends + 16)]
-    pairs = [(s, 2 - 3 * parity, 3 * s - 1, 1 - parity, s) for s in range(2)]
-    near_blocks(flags, tpos, slots, pairs, acc, scratch)
-
-
-def near(kernel, name, n_slots, n_pairs, operands, more=(), chained=True):
+    pairs += [(2 + s, 2 - 3 * parity, 3 * s - 1, 1 - parity, s) for s in range(2)]
+    near_blocks(flags, place8, slots, pairs, before, out, scratch)
+
+
+def near(kernel, name, n_slots, n_pairs, operands, chained=True, cost=None):
     return pl.pallas_call(
         kernel,
-        in_specs=[scalars] + [whole] * (len(operands) - 1),
-        out_specs=[whole] * (1 + len(more)),
-        out_shape=[ACC, *more],
+        in_specs=[scalars] + [whole] * (len(operands) - 2) + [hbm if chained else whole],
+        out_specs=[hbm],
+        out_shape=[ACC],
         scratch_shapes=near_scratch(n_slots, n_pairs),
         input_output_aliases={len(operands) - 1: 0} if chained else {},
         compiler_params=params(),
-        cost_estimate=COST,
+        cost_estimate=cost or COST,
         name=name,
     )(*operands)
 
@@ -326,33 +353,49 @@
 
 
 def far_kernel(
-    n_lat, n_lon, flags, weights, own, left, right, from_y, from_c, every, dev_w, dev_t, group_w,
-    leaf_t, out, group_row_w,
+    n_lat, n_lon, flags, weights, own, left, right, from_y, from_c, dev_a, dev_b, c_ends,
+    dev_w, dev_t, group_w, leaf_t, out, group_row_w, sem,
 ):
     lat = lax.axis_index("lat")
     lon = lax.axis_index("lon")
     parity = lax.rem(lat, 2)
+    side = lax.rem(lon, 2)
     group_row, group_col = lat // 2, lon // 2
     n_gcol = n_lon // 2
-    pltpu.sync_copy(group_w.at[group_row, group_col], group_row_w)
+    copy = pltpu.make_async_copy(group_w.at[group_row, group_col], group_row_w, sem.at[0])
+    copy.start()
+    size = n_lon * RANK
+    rows_of = ((dev_a, 0), (c_ends, 2 * MSG), (dev_b, 0), (c_ends, 2 * MSG + size))
+
+    def device_coef(k, back, col_side):
+        ref, offset = rows_of[k]
+        which = jnp.where(side == col_side, 0, 1)
+        start = pl.multiple_of(offset + (2 * back + which) * RANK, 8)
+        return ref[pl.ds(start, RANK), :]
+
     total = jnp.zeros((RANK, COLS), f32)
-    for other in range(n_lat):
+    for k in range(n_lat):
+        other = lat + k - 2 * (lat & k)
         u = other + 2 - 2 * group_row
         for v in range(6):
             shift = 2 * group_col - 2 + v
-            col = lax.rem(shift + n_lon, n_lon)
             drop = (jnp.abs(other - lat) <= 1) & (jnp.abs(shift - lon) <= 1)
             scale = jnp.where(drop, 0.0, 1.0)
-            total = total + scale * mm2(dev_w[6 * u + v], every[other * n_lon + col])
+            coef = device_coef(k, (1 - v // 2) % n_gcol, v % 2)
+            total = total + scale * mm2(dev_w[6 * u + v], coef)
+    copy.wait()
 
     def group_step(step, field):
         gcol = lax.rem(group_col + step, n_gcol)
-        for grow in range(n_lat // 2):
+        for pair in range(n_lat // 2):
+            grow = group_row + pair - 2 * (group_row & pair)
             coef = jnp.zeros((RANK, COLS), f32)
             for e in range(2):
+                k = 2 * pair + e
+                other = lat + k - 2 * (lat & k)
                 for f in range(2):
-                    cell = (2 * grow + e) * n_lon + 2 * gcol + f
-                    coef = coef + mm3(dev_t[cell], every[cell], (0, 0))
+                    cell = other * n_lon + 2 * gcol + f
+                    coef = coef + mm3(dev_t[cell], device_coef(k, n_gcol - step, f), (0, 0))
             field = field + mm2(group_row_w[grow, gcol], coef)
         return field
 
@@ -364,7 +407,7 @@
         (
             (2, ((left, PTS), (own, PTS), (right, PTS))),
             (4 * parity, (None, (from_y, 2 * PTS), None)),
-            (4 - 4 * parity, (None, (from_c, 2 * PTS), None)),
+            (4 - 4 * parity, ((c_ends, 0), (from_c, 2 * PTS), (c_ends, MSG))),
         ),
     )
     for leaf in range(4):
@@ -373,39 +416,40 @@
 
 
 def far_field(n_lat, n_lon, operands):
-    specs = [scalars] + [whole] * 11
-    specs[10] = pl.BlockSpec(memory_space=pl.ANY)
+    specs = [scalars] + [whole] * 13
+    specs[12] = hbm
     return pl.pallas_call(
         functools.partial(far_kernel, n_lat, n_lon),
         in_specs=specs,
         out_specs=whole,
         out_shape=shape(QUAD, COLS),
-        scratch_shapes=[VMEM((n_lat // 2, n_lon // 2, RANK, RANK), bf16)],
+        scratch_shapes=[
+            VMEM((n_lat // 2, n_lon // 2, RANK, RANK), bf16),
+            pltpu.SemaphoreType.DMA((1,)),
+        ],
         compiler_params=params(),
-        cost_estimate=COST,
+        cost_estimate=LOW,
         name="far",
     )(*operands)
 
 
 def down_kernel(
-    flags, tpos, weights, left_y, right_y, c_ends, partial, basis, before, acc, *scratch
+    flags, place8, weights, left_y, right_y, partial, basis, before, out, *scratch
 ):
-    acc[...] = before[...]
     parity = lat_parity()
     far = partial[...] + window_sum(
-        flags,
-        weights,
-        (
-            (4 * parity, ((left_y, PTS), None, (right_y, PTS))),
-            (4 - 4 * parity, ((c_ends, 0), None, (c_ends, QUAD))),
-        ),
-    )
-    for leaf in range(4):
-        acc[leaf] += mm3(basis[leaf], far[leaf * RANK : (leaf + 1) * RANK, :], (0, 0))
+        flags, weights, ((4 * parity, ((left_y, PTS), None, (right_y, PTS))),)
+    )
+    acc = scratch[6]
+
+    def fill(_):
+        for leaf in range(4):
+            acc[leaf] += mm3(basis[leaf], far[leaf * RANK : (leaf + 1) * RANK, :], (0, 0))
+
     base = PTS + QUAD + 8 - 8 * parity
     slots = [(left_y[:PTS, :], left_y, base + 4), (right_y[:PTS, :], right_y, base)]
     pairs = [(s, 3 * parity - 1, 3 * s - 1, parity, s) for s in range(2)]
-    near_blocks(flags, tpos, slots, pairs, acc, scratch)
+    near_blocks(flags, place8, slots, pairs, before, out, scratch, fill)
 
 
 def local(
@@ -434,35 +478,44 @@
     across = [(i, i + 1 if i % 2 else i - 1) for i in range(n_lat)]
     across = [(a, b) for a, b in across if 0 <= b < n_lat]
 
-    a_right, a_left, b_right, b_left, to_y, to_c, tpos, dev = coefficients(
+    across_two = [(i, i ^ 2) for i in range(n_lat)]
+    partner = [(i, i ^ 1) for i in range(n_lon)]
+    barrier = lax.optimization_barrier
+
+    a_right, a_left, b_right, b_left, to_y, to_c, place8, dev = coefficients(
         flat, basis, transfer, positions.reshape(4, 2, PTS)
     )
+    dev_pair = lax.ppermute(dev, "lon", partner)
     left = lax.ppermute(a_right, "lon", to_right)
     right = lax.ppermute(a_left, "lon", to_left)
+    from_c = lax.ppermute(to_c, "lat", in_chip)
+    from_y = lax.ppermute(to_y, "lat", across)
+
+    dev_a = jnp.concatenate([dev, dev_pair], 0)
+    step = 2
+    moved = lax.ppermute(dev_a, "lon", [(i, (i + step) % n_lon) for i in range(n_lon)])
+    moved, from_c, place8 = barrier((moved, from_c, place8))
+    (acc,) = near(own_kernel, "own", 4, 16, (flags, place8, flat, a_right), chained=False)
+    from_y, dev_a, acc = barrier((from_y, dev_a, acc))
+    dev_a = jnp.concatenate([dev_a, moved], 0)
+    while 2 * step < n_lon:
+        step *= 2
+        moved = lax.ppermute(dev_a, "lon", [(i, (i + step) % n_lon) for i in range(n_lon)])
+        dev_a = jnp.concatenate([dev_a, moved], 0)
+    (acc,) = near(lat_kernel, "lat", 4, 8, (flags, place8, from_y, from_c, acc))
+    dev_a, acc = barrier((dev_a, acc))
+    dev_b = lax.ppermute(dev_a, "lat", across_two)
+    left, right, dev_b, b_right, b_left, acc = barrier(
+        (left, right, dev_b, b_right, b_left, acc)
+    )
     left_b = lax.ppermute(b_right, "lon", to_right)
     right_b = lax.ppermute(b_left, "lon", to_left)
-    from_y = lax.ppermute(to_y, "lat", across)
-
-    every = lax.all_gather(dev, "lon")
-
-    (acc,) = near(own_kernel, "own", 4, 16, (flags, tpos, flat, a_right), chained=False)
-    to_c, from_y, every, acc = lax.optimization_barrier((to_c, from_y, every, acc))
-    from_c = lax.ppermute(to_c, "lat", in_chip)
-    every = lax.all_gather(every, "lat").reshape(n_lat * n_lon, RANK, COLS)
-    (acc,) = near(
-        functools.partial(lat_kernel, False), "lat_y", 2, 4, (flags, tpos, from_y, acc)
-    )
-    (acc,) = near(
-        functools.partial(lat_kernel, True), "lat_c", 2, 4, (flags, tpos, from_c, acc)
-    )
-    left, right, acc = lax.optimization_barrier((left, right, acc))
     left_y = lax.ppermute(left, "lat", across)
     right_y = lax.ppermute(right, "lat", across)
-    acc, to_c = near(
-        lon_kernel, "lon", 2, 4, (flags, tpos, left, right, acc), more=[shape(2 * MSG, COLS)]
-    )
-    every, acc = lax.optimization_barrier((every, acc))
+    to_c = jnp.concatenate([left[PTS:], right[PTS:], dev_a, dev_b], 0)
     c_ends = lax.ppermute(to_c, "lat", in_chip)
+    (acc,) = near(lon_kernel, "lon", 2, 4, (flags, place8, left, right, acc))
+    c_ends, acc = barrier((c_ends, acc))
     partial = far_field(
         n_lat,
         n_lon,
@@ -474,30 +527,33 @@
             right,
             from_y,
             from_c,
-            every,
+            dev_a,
+            dev_b,
+            c_ends,
             device_coupling.reshape(36, RANK, RANK),
             device_transfer.reshape(n_lat * n_lon, RANK, RANK),
             group_coupling,
             transfer,
         ),
     )
-    left_y, right_y, partial = lax.optimization_barrier((left_y, right_y, partial))
+    left_y, right_y, partial = barrier((left_y, right_y, partial))
     (acc,) = near(
         down_kernel,
         "down",
         2,
         2,
-        (flags, tpos, weights, left_y, right_y, c_ends, partial, basis, acc),
-    )
-    left_b, right_b, acc = lax.optimization_barrier((left_b, right_b, acc))
+        (flags, place8, weights, left_y, right_y, partial, basis, acc),
+        cost=LOW,
+    )
+    left_b, right_b, acc = barrier((left_b, right_b, acc))
     left_c = lax.ppermute(left_b, "lat", in_chip)
     right_c = lax.ppermute(right_b, "lat", in_chip)
     (acc,) = near(
-        last_kernel, "last", 2, 4, (flags, tpos, left, right, left_b, right_b, acc)
-    )
-    left_c, right_c, acc = lax.optimization_barrier((left_c, right_c, acc))
-    (acc,) = near(
-        corner_kernel, "corner", 2, 2, (flags, tpos, c_ends, left_c, right_c, acc)
+        last_kernel,
+        "last",
+        4,
+        6,
+        (flags, place8, left, right, left_b, right_b, c_ends, left_c, right_c, acc),
     )
     return acc.reshape(2, 2, PTS, COLS)
 

time: 311 us -> 114 us (0.37)
  the two profiles are of different devices: /device:TPU:9 before, /device:TPU:1 now
where the time goes in v2:
time: 114 us; the launch traced here: 112 us
  Pallas kernels  56.9 us (50%)
  waiting for transfers between devices  23.3 us (20%)
  starting transfers between devices  23 us (20%)
  local copies, waits for them, and re-layouts  4.3 us (4%)
  other arithmetic  4.02 us (4%)
    pallas_call x5, Pallas kernels, near(): pl.pallas_call(kernel, in_specs=[scalars] + [whole] * (len(operands) - 2)...  41.8 us
    ppermute x1, waiting for transfers between devices, local(): dev_b = lax.ppermute(dev_a, 'lat', across_two)  10.6 us
    pallas_call x1, Pallas kernels, far_field(): pl.pallas_call(functools.partial(far_kernel, n_lat, n_lon), in_specs=spec...  9.44 us
    ppermute x2, waiting for transfers between devices, local(): lax.ppermute(dev_a, 'lon', [(i, (i + step) % n_lon) for i in range(n_lon)])  5.77 us
    pallas_call x1, Pallas kernels, coefficients(): pl.pallas_call(coef_kernel, in_specs=[hbm, hbm, whole, whole], out_specs=...  5.73 us
    ppermute x1, starting transfers between devices, local(): from_y = lax.ppermute(to_y, 'lat', across)  4.15 us
    ppermute x1, starting transfers between devices, local(): right_b = lax.ppermute(b_left, 'lon', to_left)  4.15 us
    ppermute x1, starting transfers between devices, local(): right = lax.ppermute(a_left, 'lon', to_left)  2.95 us
  transfers between devices with their start and end apart: 15, of which 7 were waited for; matrix products, arithmetic and copies ran while one was open for 5% of the time, Pallas kernels for 39%

profile of v2, /device:TPU:1, one launch (start us, length us, event | category | flops | bytes accessed | tf_op | source)
XLA Modules:
  0.0 111.9 jit_solution(9047785303150456550)
XLA Ops:
  0.0 5.7 %coefs.1 = (f32[784,256]{1,0:T(8,128)}, f32[784,256]{1,0:T(8,128)}, f32[512,256]{1,0:T(8,128)}, f32[512,256]{1,0:T(8,128)}, f32[1296,256]{1,0:T(8,128)}, /*index...) custom-call(f32[4,512,256]{2,1,0:T(8,128)} %bitcast.25, f32[4,64,512]{2,1,0:T(8,128)} %bitcast.15, ...), custom_call_target="tpu_custom_call" | custom-call | flops 20000000000 | bytes 4000000 | tf_op jit(solution)/shard_map/coefs/pallas_call | solution.py:130
  5.7 0.1 collective-permute-start.2
  5.9 2.7 %collective-permute-start = (f32[64,256]{1,0:T(8,128)}, f32[64,256]{1,0:T(8,128)S(1)}, u32[]{:S(2)}, u32[]{:S(2)}) collective-permute-start(f32[64,256]{1,0:T(8,128)} %get-tuple-element.35), channel_id=1, source_target_pairs={{0,1},{1,0},{2,3},{3,2},{4,5},{5,4},{6,7},{7,6},{8,9},{9,8},{10,11... | collective-permute-start | bytes 196616 | tf_op jit(solution)/shard_map/ppermute | solution.py:488
  8.5 0.9 constant_dynamic-update-slice_fusion.1
  9.4 1.7 %collective-permute-done = f32[64,256]{1,0:T(8,128)S(1)} collective-permute-done((f32[64,256]{1,0:T(8,128)}, f32[64,256]{1,0:T(8,128)S(1)}, u32[]{:S(2)}, u32[]{:S(2)}) %collective-permute-start) | collective-permute-done | bytes 65568 | tf_op jit(solution)/shard_map/ppermute | solution.py:488
  11.1 0.7 copy-done.2
  11.8 1.4 %collective-permute-start.1 = (f32[128,256]{1,0:T(8,128)S(1)}, f32[128,256]{1,0:T(8,128)S(1)}, u32[]{:S(2)}, u32[]{:S(2)}) collective-permute-start(f32[128,256]{1,0:T(8,128)S(1)} %constant_dynamic-update-slice_fusion), channel_id=1, source_target_pairs={{0,2},{1,3},{2,4},{3,5},{4,6},{5,7},{6,0},{7,1},{8,10},{9,11},{10,... | collective-permute-start | bytes 393224 | tf_op jit(solution)/shard_map/ppermute | solution.py:496
  13.1 4.2 %collective-permute-start.5 = (f32[1296,256]{1,0:T(8,128)}, f32[1296,256]{1,0:T(8,128)}, u32[]{:S(2)}, u32[]{:S(2)}) collective-permute-start(f32[1296,256]{1,0:T(8,128)} %get-tuple-element.41), channel_id=1, source_target_pairs={{8,16},{16,8},{9,17},{17,9},{10,18},{18,10},{11,19},{19,11},{12,20... | collective-permute-start | bytes 3981320 | tf_op jit(solution)/shard_map/ppermute | solution.py:492
  17.3 1.3 %collective-permute-start.3 = (f32[784,256]{1,0:T(8,128)}, f32[784,256]{1,0:T(8,128)}, u32[]{:S(2)}, u32[]{:S(2)}) collective-permute-start(f32[784,256]{1,0:T(8,128)} %get-tuple-element.39.msg.own), channel_id=1, source_target_pairs={{0,1},{1,2},{2,3},{3,4},{4,5},{5,6},{6,7},{7,0},{8,9},{9,10},{10,1... | collective-permute-start | bytes 2408456 | tf_op jit(solution)/shard_map/ppermute | solution.py:489
  18.6 3.0 %collective-permute-start.4 = (f32[784,256]{1,0:T(8,128)}, f32[784,256]{1,0:T(8,128)}, u32[]{:S(2)}, u32[]{:S(2)}) collective-permute-start(f32[784,256]{1,0:T(8,128)} %get-tuple-element.40), channel_id=1, source_target_pairs={{0,7},{1,0},{2,1},{3,2},{4,3},{5,4},{6,5},{7,6},{8,15},{9,8},{10,9... | collective-permute-start | bytes 2408456 | tf_op jit(solution)/shard_map/ppermute | solution.py:490
  21.5 0.6 copy-done.3
  22.2 15.2 %own.1.before = f32[4,512,256]{2,1,0:T(8,128)} custom-call(s32[4,9]{1,0:T(4,128)} %bitcast.19, f32[4,8,512]{2,1,0:T(8,128)} %get-tuple-element.38.place8, f32[4,512,256]{2,1,0:T(8,128)} %bitcast.26, f32[784,256]{1,0:T(8,128)} %get-tuple-element.39.msg.own), custom_call_target="tpu_custom_call" | custom-call | flops 20000000000 | bytes 4000000 | tf_op jit(solution)/shard_map/own/pallas_call | solution.py:313
  37.4 1.7 %pad_maximum_fusion.2 = f32[256,256]{1,0:T(8,128)} fusion(f32[128,256]{1,0:T(8,128)} %copy-done.3, f32[128,256]{1,0:T(8,128)} %copy-done.2), kind=kLoop, calls=%fused_computation.2 | loop fusion | flops 65536 | bytes 524288 | tf_op jit(solution)/shard_map/concatenate | solution.py:500
  39.1 6.4 %lat.1.before = f32[4,512,256]{2,1,0:T(8,128)} custom-call(s32[4,9]{1,0:T(4,128)} %bitcast.20, f32[4,8,512]{2,1,0:T(8,128)} %get-tuple-element.38.place8, f32[1296,256]{1,0:T(8,128)} %collective-permute-done.5.from_y, f32[1296,256]{1,0:T(8,128)} %collective-permute-done.2.from_c, f32[4,512,256]{2,1,0:T(8,128)} %own.1.before), custom_call_target="tpu_custom_call", output_to_operand_aliasing={{}: (4, {})} | custom-call | flops 20000000000 | bytes 4000000 | tf_op jit(solution)/shard_map/lat/pallas_call | solution.py:313
  45.4 5.8 %collective-permute-done.6 = f32[256,256]{1,0:T(8,128)} collective-permute-done((f32[256,256]{1,0:T(8,128)}, f32[256,256]{1,0:T(8,128)}, u32[]{:S(2)}, u32[]{:S(2)}) %collective-permute-start.6) | collective-permute-done | bytes 262176 | tf_op jit(solution)/shard_map/ppermute | solution.py:503
  51.2 1.1 pad_maximum_fusion.1.dev_a
  52.4 0.6 collective-permute-done.3.left.a_left
  52.9 2.2 %collective-permute-done.4.right.a_right = f32[784,256]{1,0:T(8,128)} collective-permute-done((f32[784,256]{1,0:T(8,128)}, f32[784,256]{1,0:T(8,128)}, u32[]{:S(2)}, u32[]{:S(2)}) %collective-permute-start.4) | collective-permute-done | bytes 802848 | tf_op jit(solution)/shard_map/ppermute | solution.py:490
  55.1 10.6 %collective-permute-done.7.dev_b = f32[512,256]{1,0:T(8,128)S(1)} collective-permute-done((f32[512,256]{1,0:T(8,128)S(1)}, f32[512,256]{1,0:T(8,128)S(1)}, u32[]{:S(2)}, u32[]{:S(2)}) %collective-permute-start.7) | collective-permute-done | bytes 524320 | tf_op jit(solution)/shard_map/ppermute | solution.py:507
  65.7 1.1 %slice.6 = f32[272,256]{1,0:T(8,128)S(1)} slice(f32[784,256]{1,0:T(8,128)} %collective-permute-done.3.left.a_left), slice={[512:784], [0:256]} | slice | bytes 557056 | tf_op jit(solution)/shard_map/slice | solution.py:515
  66.9 2.8 %collective-permute-start.10 = (f32[784,256]{1,0:T(8,128)}, f32[784,256]{1,0:T(8,128)}, u32[]{:S(2)}, u32[]{:S(2)}) collective-permute-start(f32[784,256]{1,0:T(8,128)} %collective-permute-done.3.left.a_left), channel_id=1, source_target_pairs={{8,16},{16,8},{9,17},{17,9},{10,18},{18,10},{11,19},{19,11},{12,20... | collective-permute-start | bytes 2408456 | tf_op jit(solution)/shard_map/ppermute | solution.py:513
  69.7 1.0 slice.7
  70.6 2.8 %collective-permute-start.11 = (f32[784,256]{1,0:T(8,128)}, f32[784,256]{1,0:T(8,128)}, u32[]{:S(2)}, u32[]{:S(2)}) collective-permute-start(f32[784,256]{1,0:T(8,128)} %collective-permute-done.4.right.a_right), channel_id=1, source_target_pairs={{8,16},{16,8},{9,17},{17,9},{10,18},{18,10},{11,19},{19,11},{12,20... | collective-permute-start | bytes 2408456 | tf_op jit(solution)/shard_map/ppermute | solution.py:514
  73.4 1.2 %pad_maximum_fusion = f32[1568,256]{1,0:T(8,128)} fusion(f32[512,256]{1,0:T(8,128)S(1)} %collective-permute-done.7.dev_b, f32[512,256]{1,0:T(8,128)S(1)} %pad_maximum_fusion.1.dev_a, f32[272,256]{1,0:T(8,128)S(1)} %slice.7, f32[272,256]{1,0:T(8,128)S(1)} %slice.6), kind=kLoop, calls=%fused_computation | loop fusion | flops 1204224 | bytes 3211264 | tf_op jit(solution)/shard_map/concatenate | solution.py:515
  74.8 4.1 %collective-permute-start.9 = (f32[512,256]{1,0:T(8,128)}, f32[512,256]{1,0:T(8,128)}, u32[]{:S(2)}, u32[]{:S(2)}) collective-permute-start(f32[512,256]{1,0:T(8,128)} %get-tuple-element.54), channel_id=1, source_target_pairs={{0,7},{1,0},{2,1},{3,2},{4,3},{5,4},{6,5},{7,6},{8,15},{9,8},{10,9... | collective-permute-start | bytes 1572872 | tf_op jit(solution)/shard_map/ppermute | solution.py:512
  78.9 5.3 %lon.1.before = f32[4,512,256]{2,1,0:T(8,128)} custom-call(s32[4,9]{1,0:T(4,128)} %bitcast.21, f32[4,8,512]{2,1,0:T(8,128)} %get-tuple-element.38.place8, f32[784,256]{1,0:T(8,128)} %collective-permute-done.3.left.a_left, f32[784,256]{1,0:T(8,128)} %collective-permute-done.4.right.a_right, f32[4,512,256]{2,1,0:T(8,128)} %lat.1.before), custom_call_target="tpu_custom_call", output_to_operand_aliasing={{}: (4, {})} | custom-call | flops 20000000000 | bytes 4000000 | tf_op jit(solution)/shard_map/lon/pallas_call | solution.py:313
  84.3 9.4 %far.1.partial = f32[256,256]{1,0:T(8,128)} custom-call(s32[4,9]{1,0:T(4,128)} %bitcast.22, bf16[4,36,64,64]{3,2,1,0:T(8,128)(2,1)} %bitcast.11, f32[784,256]{1,0:T(8,128)} %get-tuple-element.39.msg.own, f32[784,256]{1,0:T(8,128)} %collective-permute-done.3.left.a_left, f32[784,256]{1,0:T(8,128)} %collective-permute-done.4.right.a_right, ...), custom_call_target="tpu_custom_call" | custom-call | flops 1000 | bytes 1000 | tf_op jit(solution)/shard_map/far/pallas_call | solution.py:421
  93.8 7.8 %down.1.before = f32[4,512,256]{2,1,0:T(8,128)} custom-call(s32[4,9]{1,0:T(4,128)} %bitcast.23, f32[4,8,512]{2,1,0:T(8,128)} %get-tuple-element.38.place8, bf16[4,36,64,64]{3,2,1,0:T(8,128)(2,1)} %bitcast.12, f32[784,256]{1,0:T(8,128)} %collective-permute-done.10.left_y, f32[784,256]{1,0:T(8,128)} %collective-permute-done.11.right_y, ...), custom_call_target="tpu_custom_call", output_to_operand_aliasing={{}: (7, {})} | custom-call | flops 1000 | bytes 1000 | tf_op jit(solution)/shard_map/down/pallas_call | solution.py:313
  101.6 0.5 collective-permute-start.14
  102.1 1.7 %collective-permute-done.13.left_c = f32[512,256]{1,0:T(8,128)} collective-permute-done((f32[512,256]{1,0:T(8,128)}, f32[512,256]{1,0:T(8,128)}, u32[]{:S(2)}, u32[]{:S(2)}) %collective-permute-start.13) | collective-permute-done | bytes 524320 | tf_op jit(solution)/shard_map/ppermute | solution.py:549
  103.9 0.7 collective-permute-done.14.right_c
  104.6 7.1 %last.1 = f32[4,512,256]{2,1,0:T(8,128)} custom-call(s32[4,9]{1,0:T(4,128)} %bitcast.24, f32[4,8,512]{2,1,0:T(8,128)} %get-tuple-element.38.place8, f32[784,256]{1,0:T(8,128)} %collective-permute-done.3.left.a_left, f32[784,256]{1,0:T(8,128)} %collective-permute-done.4.right.a_right, ...), custom_call_target="tpu_custom_call", output_to_operand_aliasing={{}: (9, {})} | custom-call | flops 20000000000 | bytes 4000000 | tf_op jit(solution)/shard_map/last/pallas_call | solution.py:313
  (20 shorter events, 0.2 us)
Async XLA Ops:
  5.7 16.4 %collective-permute-start.2 = (f32[1296,256]{1,0:T(8,128)}, f32[1296,256]{1,0:T(8,128)}, u32[]{:S(2)}, u32[]{:S(2)}) collective-permute-start(f32[1296,256]{1,0:T(8,128)} %get-tuple-element.36), channel_id=1, source_target_pairs={{0,8},{8,0},{16,24},{24,16},{1,9},{9,1},{17,25},{25,17},{2,10},{10... | collective-permute-start | bytes 3981320 | tf_op jit(solution)/shard_map/ppermute | solution.py:491
  5.9 5.3 %collective-permute-start = (f32[64,256]{1,0:T(8,128)}, f32[64,256]{1,0:T(8,128)S(1)}, u32[]{:S(2)}, u32[]{:S(2)}) collective-permute-start(f32[64,256]{1,0:T(8,128)} %get-tuple-element.35), channel_id=1, source_target_pairs={{0,1},{1,0},{2,3},{3,2},{4,5},{5,4},{6,7},{7,6},{8,9},{9,8},{10,11... | collective-permute-start | bytes 196616 | tf_op jit(solution)/shard_map/ppermute | solution.py:488
  11.1 0.7 copy-start.2
  11.8 9.8 %collective-permute-start.1 = (f32[128,256]{1,0:T(8,128)S(1)}, f32[128,256]{1,0:T(8,128)S(1)}, u32[]{:S(2)}, u32[]{:S(2)}) collective-permute-start(f32[128,256]{1,0:T(8,128)S(1)} %constant_dynamic-update-slice_fusion), channel_id=1, source_target_pairs={{0,2},{1,3},{2,4},{3,5},{4,6},{5,7},{6,0},{7,1},{8,10},{9,11},{10,... | collective-permute-start | bytes 393224 | tf_op jit(solution)/shard_map/ppermute | solution.py:496
  13.1 24.2 %collective-permute-start.5 = (f32[1296,256]{1,0:T(8,128)}, f32[1296,256]{1,0:T(8,128)}, u32[]{:S(2)}, u32[]{:S(2)}) collective-permute-start(f32[1296,256]{1,0:T(8,128)} %get-tuple-element.41), channel_id=1, source_target_pairs={{8,16},{16,8},{9,17},{17,9},{10,18},{18,10},{11,19},{19,11},{12,20... | collective-permute-start | bytes 3981320 | tf_op jit(solution)/shard_map/ppermute | solution.py:492
  17.3 35.6 %collective-permute-start.3 = (f32[784,256]{1,0:T(8,128)}, f32[784,256]{1,0:T(8,128)}, u32[]{:S(2)}, u32[]{:S(2)}) collective-permute-start(f32[784,256]{1,0:T(8,128)} %get-tuple-element.39.msg.own), channel_id=1, source_target_pairs={{0,1},{1,2},{2,3},{3,4},{4,5},{5,6},{6,7},{7,0},{8,9},{9,10},{10,1... | collective-permute-start | bytes 2408456 | tf_op jit(solution)/shard_map/ppermute | solution.py:489
  18.6 36.6 %collective-permute-start.4 = (f32[784,256]{1,0:T(8,128)}, f32[784,256]{1,0:T(8,128)}, u32[]{:S(2)}, u32[]{:S(2)}) collective-permute-start(f32[784,256]{1,0:T(8,128)} %get-tuple-element.40), channel_id=1, source_target_pairs={{0,7},{1,0},{2,1},{3,2},{4,3},{5,4},{6,5},{7,6},{8,15},{9,8},{10,9... | collective-permute-start | bytes 2408456 | tf_op jit(solution)/shard_map/ppermute | solution.py:490
  21.5 0.6 copy-start.3
  39.1 12.2 %collective-permute-start.6 = (f32[256,256]{1,0:T(8,128)}, f32[256,256]{1,0:T(8,128)}, u32[]{:S(2)}, u32[]{:S(2)}) collective-permute-start(f32[256,256]{1,0:T(8,128)} %pad_maximum_fusion.2), channel_id=1, source_target_pairs={{0,4},{1,5},{2,6},{3,7},{4,0},{5,1},{6,2},{7,3},{8,12},{9,13},{10,... | collective-permute-start | bytes 786440 | tf_op jit(solution)/shard_map/ppermute | solution.py:503
  52.3 22.4 %copy-start = (f32[512,256]{1,0:T(8,128)}, f32[512,256]{1,0:T(8,128)S(1)}, u32[]{:S(2)}) copy-start(f32[512,256]{1,0:T(8,128)S(1)} %pad_maximum_fusion.1.dev_a) | copy-start | bytes 1572868
  52.3 13.4 %collective-permute-start.7 = (f32[512,256]{1,0:T(8,128)S(1)}, f32[512,256]{1,0:T(8,128)S(1)}, u32[]{:S(2)}, u32[]{:S(2)}) collective-permute-start(f32[512,256]{1,0:T(8,128)S(1)} %pad_maximum_fusion.1.dev_a), channel_id=1, source_target_pairs={{0,16},{8,24},{16,0},{24,8},{1,17},{9,25},{17,1},{25,9},{2,18},{10... | collective-permute-start | bytes 1572872 | tf_op jit(solution)/shard_map/ppermute | solution.py:507
  65.7 9.0 %copy-start.1 = (f32[512,256]{1,0:T(8,128)}, f32[512,256]{1,0:T(8,128)S(1)}, u32[]{:S(2)}) copy-start(f32[512,256]{1,0:T(8,128)S(1)} %collective-permute-done.7.dev_b) | copy-start | bytes 1572868
  66.9 26.9 %collective-permute-start.10 = (f32[784,256]{1,0:T(8,128)}, f32[784,256]{1,0:T(8,128)}, u32[]{:S(2)}, u32[]{:S(2)}) collective-permute-start(f32[784,256]{1,0:T(8,128)} %collective-permute-done.3.left.a_left), channel_id=1, source_target_pairs={{8,16},{16,8},{9,17},{17,9},{10,18},{18,10},{11,19},{19,11},{12,20... | collective-permute-start | bytes 2408456 | tf_op jit(solution)/shard_map/ppermute | solution.py:513
  70.6 23.1 %collective-permute-start.11 = (f32[784,256]{1,0:T(8,128)}, f32[784,256]{1,0:T(8,128)}, u32[]{:S(2)}, u32[]{:S(2)}) collective-permute-start(f32[784,256]{1,0:T(8,128)} %collective-permute-done.4.right.a_right), channel_id=1, source_target_pairs={{8,16},{16,8},{9,17},{17,9},{10,18},{18,10},{11,19},{19,11},{12,20... | collective-permute-start | bytes 2408456 | tf_op jit(solution)/shard_map/ppermute | solution.py:514
  74.7 9.6 %collective-permute-start.12 = (f32[1568,256]{1,0:T(8,128)}, f32[1568,256]{1,0:T(8,128)}, u32[]{:S(2)}, u32[]{:S(2)}) collective-permute-start(f32[1568,256]{1,0:T(8,128)} %pad_maximum_fusion), channel_id=1, source_target_pairs={{0,8},{8,0},{16,24},{24,16},{1,9},{9,1},{17,25},{25,17},{2,10},{10... | collective-permute-start | bytes 4816904 | tf_op jit(solution)/shard_map/ppermute | solution.py:516
  74.7 26.8 %collective-permute-start.8 = (f32[512,256]{1,0:T(8,128)}, f32[512,256]{1,0:T(8,128)}, u32[]{:S(2)}, u32[]{:S(2)}) collective-permute-start(f32[512,256]{1,0:T(8,128)} %get-tuple-element.53), channel_id=1, source_target_pairs={{0,1},{1,2},{2,3},{3,4},{4,5},{5,6},{6,7},{7,0},{8,9},{9,10},{10,1... | collective-permute-start | bytes 1572872 | tf_op jit(solution)/shard_map/ppermute | solution.py:511
  74.8 26.8 %collective-permute-start.9 = (f32[512,256]{1,0:T(8,128)}, f32[512,256]{1,0:T(8,128)}, u32[]{:S(2)}, u32[]{:S(2)}) collective-permute-start(f32[512,256]{1,0:T(8,128)} %get-tuple-element.54), channel_id=1, source_target_pairs={{0,7},{1,0},{2,1},{3,2},{4,3},{5,4},{6,5},{7,6},{8,15},{9,8},{10,9... | collective-permute-start | bytes 1572872 | tf_op jit(solution)/shard_map/ppermute | solution.py:512
  101.5 2.3 %collective-permute-start.13 = (f32[512,256]{1,0:T(8,128)}, f32[512,256]{1,0:T(8,128)}, u32[]{:S(2)}, u32[]{:S(2)}) collective-permute-start(f32[512,256]{1,0:T(8,128)} %collective-permute-done.8.left), channel_id=1, source_target_pairs={{0,8},{8,0},{16,24},{24,16},{1,9},{9,1},{17,25},{25,17},{2,10},{10... | collective-permute-start | bytes 1572872 | tf_op jit(solution)/shard_map/ppermute | solution.py:549
  101.6 3.0 %collective-permute-start.14 = (f32[512,256]{1,0:T(8,128)}, f32[512,256]{1,0:T(8,128)}, u32[]{:S(2)}, u32[]{:S(2)}) collective-permute-start(f32[512,256]{1,0:T(8,128)} %collective-permute-done.9.right), channel_id=1, source_target_pairs={{0,8},{8,0},{16,24},{24,16},{1,9},{9,1},{17,25},{25,17},{2,10},{10... | collective-permute-start | bytes 1572872 | tf_op jit(solution)/shard_map/ppermute | solution.py:550

commit v3 on v2

--- a/solution.py
+++ b/solution.py
@@ -163,12 +163,23 @@
         VMEM((PTS, 2 * PTS), bf16),
         VMEM((PTS, 2 * PTS), bf16),
         VMEM((4, PTS, COLS), f32),
-        pltpu.SemaphoreType.DMA((8,)),
+        VMEM((n_slots, PTS, COLS), f32),
+        VMEM((n_slots, 16, COLS), f32),
+        pltpu.SemaphoreType.DMA((8 + 2 * n_slots,)),
     ]
 
 
 def near_blocks(flags, place8, slots, pairs, before, out, scratch, fill=None):
-    table, tpos, spos, stack, kern_a, kern_b, acc, sems = scratch
+    table, tpos, spos, stack, kern_a, kern_b, acc, stage, marks, sems = scratch
+    arrivals = []
+    for slot, (values, places, _) in enumerate(slots):
+        pair = (
+            pltpu.make_async_copy(values, stage.at[slot], sems.at[8 + 2 * slot]),
+            pltpu.make_async_copy(places, marks.at[slot], sems.at[9 + 2 * slot]),
+        )
+        for copy in pair:
+            copy.start()
+        arrivals.append(pair)
     loads = []
     if before is not None:
         loads = [
@@ -179,14 +190,16 @@
         copy.start()
     for leaf in range(4):
         tpos[leaf] = place8[leaf].T
-    for slot, (values, places, base) in enumerate(slots):
-        hi, lo = split(values)
+    for slot, (_, _, base) in enumerate(slots):
+        for copy in arrivals[slot]:
+            copy.wait()
+        hi, lo = split(stage[slot])
         stack[slot, :PTS, :] = hi
         stack[slot, PTS:, :] = lo
         for coord in range(2):
             for half in range(2):
-                spos[slot, coord : coord + 1, half * HALF : (half + 1) * HALF] = places[
-                    pl.ds(base + 2 * coord + half, 1), :
+                spos[slot, coord : coord + 1, half * HALF : (half + 1) * HALF] = marks[
+                    slot, pl.ds(base + 2 * coord + half, 1), :
                 ]
     count = 0
     for slot, row, col, own_row, own_col in pairs:
@@ -235,7 +248,7 @@
     for copy in loads:
         copy.wait()
     if fill is not None:
-        fill(acc)
+        fill(acc, stage)
 
     @pl.loop(0, (count + 1) // 2)
     def _(pair):
@@ -258,20 +271,23 @@
 ACC = shape(4, PTS, COLS)
 
 
+def block(ref, start, rows):
+    return ref.at[pl.ds(start, rows)]
+
+
 def own_kernel(flags, place8, loss, msg, out, *scratch):
-    slots = [(loss[leaf], msg, PTS + QUAD + 4 * leaf) for leaf in range(4)]
+    slots = [(loss.at[leaf], block(msg, PTS + QUAD, 16), 4 * leaf) for leaf in range(4)]
     pairs = [(s, s // 2, s % 2, t // 2, t % 2) for s in range(4) for t in range(4)]
 
-    def fill(acc):
+    def fill(acc, losses):
         for leaf in range(4):
-            acc[leaf] = 0.5 * loss[leaf]
+            acc[leaf] = 0.5 * losses[leaf]
 
     near_blocks(flags, place8, slots, pairs, None, out, scratch, fill)
 
 
 def lat_kernel(flags, place8, from_y, from_c, before, out, *scratch):
     parity = lat_parity()
-    base = 2 * PTS + QUAD
     slots, pairs = [], []
     for ref, place, row, own_row in (
         (from_y, 8 - 8 * parity, 3 * parity - 1, parity),
@@ -280,14 +296,19 @@
         for col in range(2):
             for own_col in range(2):
                 pairs.append((len(slots), row, col, own_row, own_col))
-            slots.append((ref[col * PTS : (col + 1) * PTS, :], ref, base + place + 4 * col))
+            slots.append(
+                (block(ref, col * PTS, PTS), block(ref, 2 * PTS + QUAD, 16), place + 4 * col)
+            )
     near_blocks(flags, place8, slots, pairs, before, out, scratch)
 
 
 def lon_kernel(flags, place8, left, right, before, out, *scratch):
     parity = lat_parity()
-    base = PTS + QUAD + 8 * parity
-    slots = [(left[:PTS, :], left, base + 4), (right[:PTS, :], right, base)]
+    at = PTS + QUAD
+    slots = [
+        (block(left, 0, PTS), block(left, at, 16), 8 * parity + 4),
+        (block(right, 0, PTS), block(right, at, 16), 8 * parity),
+    ]
     pairs = [(s, parity, 3 * s - 1, i, s) for s in range(2) for i in range(2)]
     near_blocks(flags, place8, slots, pairs, before, out, scratch)
 
@@ -296,26 +317,26 @@
     flags, place8, a_left, a_right, left, right, c_ends, left_c, right_c, before, out, *scratch
 ):
     parity = lat_parity()
-    base = PTS + QUAD + 8 - 8 * parity
-    ends = QUAD + 8 * parity
+    at = PTS + QUAD
+    own_place, far_place = 8 - 8 * parity, 8 * parity
     slots = [
-        (left[...], a_left, base + 4),
-        (right[...], a_right, base),
-        (left_c[...], c_ends, ends + 4),
-        (right_c[...], c_ends, MSG + ends),
+        (left, block(a_left, at, 16), own_place + 4),
+        (right, block(a_right, at, 16), own_place),
+        (left_c, block(c_ends, at, 16), far_place + 4),
+        (right_c, block(c_ends, PTS + MSG + at, 16), far_place),
     ]
     pairs = [(s, 1 - parity, 3 * s - 1, i, s) for s in range(2) for i in range(2)]
     pairs += [(2 + s, 2 - 3 * parity, 3 * s - 1, 1 - parity, s) for s in range(2)]
     near_blocks(flags, place8, slots, pairs, before, out, scratch)
 
 
-def near(kernel, name, n_slots, n_pairs, operands, chained=True, cost=None):
+def near(kernel, name, n_slots, n_pairs, operands, chained=True, cost=None, scratch=()):
     return pl.pallas_call(
         kernel,
-        in_specs=[scalars] + [whole] * (len(operands) - 2) + [hbm if chained else whole],
+        in_specs=[scalars, whole] + [hbm] * (len(operands) - 2),
         out_specs=[hbm],
         out_shape=[ACC],
-        scratch_shapes=near_scratch(n_slots, n_pairs),
+        scratch_shapes=near_scratch(n_slots, n_pairs) + list(scratch),
         input_output_aliases={len(operands) - 1: 0} if chained else {},
         compiler_params=params(),
         cost_estimate=cost or COST,
@@ -323,7 +344,7 @@
     )(*operands)
 
 
-def window_sum(flags, weights, bands):
+def window_sum(flags, weights, bands, first=0):
     total = None
     for base, cells in bands:
         for v in range(6):
@@ -337,15 +358,15 @@
                 w = 6 * u + v
                 rows = []
                 for leaf in range(4):
-                    block = weights[leaf, w]
+                    part_w = weights[leaf, w - first]
                     d_row = u - 2 - leaf // 2
                     d_col = v - 2 - leaf % 2
                     if abs(d_col) <= 1:
                         inside = (d_row >= -1) & (d_row <= 1)
                         flag = flags[leaf, 3 * jnp.clip(d_row + 1, 0, 2) + d_col + 1]
                         keep = 1 - jnp.where(inside, flag, 0)
-                        block = (block.astype(f32) * keep.astype(f32)).astype(bf16)
-                    rows.append(block)
+                        part_w = (part_w.astype(f32) * keep.astype(f32)).astype(bf16)
+                    rows.append(part_w)
                 stacked = jnp.concatenate(rows, 0)
                 part = mm(stacked, hi) + mm(stacked, lo)
                 total = part if total is None else total + part
@@ -354,7 +375,8 @@
 
 def far_kernel(
     n_lat, n_lon, flags, weights, own, left, right, from_y, from_c, dev_a, dev_b, c_ends,
-    dev_w, dev_t, group_w, leaf_t, out, group_row_w, sem,
+    dev_w, dev_t, group_w, leaf_t, out, weights_v, cells, rows_dev, dev_w_v, dev_t_v,
+    group_row_w, leaf_t_v, sems,
 ):
     lat = lax.axis_index("lat")
     lon = lax.axis_index("lon")
@@ -362,16 +384,40 @@
     side = lax.rem(lon, 2)
     group_row, group_col = lat // 2, lon // 2
     n_gcol = n_lon // 2
-    copy = pltpu.make_async_copy(group_w.at[group_row, group_col], group_row_w, sem.at[0])
-    copy.start()
     size = n_lon * RANK
-    rows_of = ((dev_a, 0), (c_ends, 2 * MSG), (dev_b, 0), (c_ends, 2 * MSG + size))
+    ends = 2 * (PTS + MSG)
+    copies = []
+    for source, target in (
+        (dev_w, dev_w_v),
+        (dev_a, rows_dev.at[0]),
+        (block(c_ends, ends, size), rows_dev.at[1]),
+        (dev_b, rows_dev.at[2]),
+        (block(c_ends, ends + size, size), rows_dev.at[3]),
+        (group_w.at[group_row, group_col], group_row_w),
+        (dev_t, dev_t_v),
+        (leaf_t, leaf_t_v),
+        (block(own, PTS, QUAD), cells.at[0]),
+        (block(left, PTS, QUAD), cells.at[1]),
+        (block(right, PTS, QUAD), cells.at[2]),
+        (block(from_y, 2 * PTS, QUAD), cells.at[3]),
+        (block(from_c, 2 * PTS, QUAD), cells.at[4]),
+        (block(c_ends, PTS, QUAD), cells.at[5]),
+        (block(c_ends, 2 * PTS + MSG, QUAD), cells.at[6]),
+        (weights.at[0], weights_v.at[0]),
+        (weights.at[1], weights_v.at[1]),
+        (weights.at[2], weights_v.at[2]),
+        (weights.at[3], weights_v.at[3]),
+    ):
+        copy = pltpu.make_async_copy(source, target, sems.at[len(copies)])
+        copy.start()
+        copies.append(copy)
+    for copy in copies[:5]:
+        copy.wait()
 
     def device_coef(k, back, col_side):
-        ref, offset = rows_of[k]
         which = jnp.where(side == col_side, 0, 1)
-        start = pl.multiple_of(offset + (2 * back + which) * RANK, 8)
-        return ref[pl.ds(start, RANK), :]
+        start = pl.multiple_of((2 * back + which) * RANK, RANK)
+        return rows_dev[k, pl.ds(start, RANK), :]
 
     total = jnp.zeros((RANK, COLS), f32)
     for k in range(n_lat):
@@ -382,8 +428,9 @@
             drop = (jnp.abs(other - lat) <= 1) & (jnp.abs(shift - lon) <= 1)
             scale = jnp.where(drop, 0.0, 1.0)
             coef = device_coef(k, (1 - v // 2) % n_gcol, v % 2)
-            total = total + scale * mm2(dev_w[6 * u + v], coef)
-    copy.wait()
+            total = total + scale * mm2(dev_w_v[6 * u + v], coef)
+    for copy in copies[5:8]:
+        copy.wait()
 
     def group_step(step, field):
         gcol = lax.rem(group_col + step, n_gcol)
@@ -395,37 +442,43 @@
                 other = lat + k - 2 * (lat & k)
                 for f in range(2):
                     cell = other * n_lon + 2 * gcol + f
-                    coef = coef + mm3(dev_t[cell], device_coef(k, n_gcol - step, f), (0, 0))
+                    coef = coef + mm3(dev_t_v[cell], device_coef(k, n_gcol - step, f), (0, 0))
             field = field + mm2(group_row_w[grow, gcol], coef)
         return field
 
     field = lax.fori_loop(2, n_gcol - 1, group_step, jnp.zeros((RANK, COLS), f32))
-    total = total + mm3(dev_t[lat * n_lon + lon], field)
+    total = total + mm3(dev_t_v[lat * n_lon + lon], field)
+    for copy in copies[8:]:
+        copy.wait()
     far = window_sum(
         flags,
-        weights,
+        weights_v,
         (
-            (2, ((left, PTS), (own, PTS), (right, PTS))),
-            (4 * parity, (None, (from_y, 2 * PTS), None)),
-            (4 - 4 * parity, ((c_ends, 0), (from_c, 2 * PTS), (c_ends, MSG))),
+            (2, tuple((cells.at[i], 0) for i in (1, 0, 2))),
+            (4 * parity, (None, (cells.at[3], 0), None)),
+            (4 - 4 * parity, tuple((cells.at[i], 0) for i in (5, 4, 6))),
         ),
     )
     for leaf in range(4):
         rows = slice(leaf * RANK, (leaf + 1) * RANK)
-        out[rows, :] = far[rows, :] + mm3(leaf_t[leaf], total)
+        out[rows, :] = far[rows, :] + mm3(leaf_t_v[leaf], total)
 
 
 def far_field(n_lat, n_lon, operands):
-    specs = [scalars] + [whole] * 13
-    specs[12] = hbm
     return pl.pallas_call(
         functools.partial(far_kernel, n_lat, n_lon),
-        in_specs=specs,
+        in_specs=[scalars] + [hbm] * 13,
         out_specs=whole,
         out_shape=shape(QUAD, COLS),
         scratch_shapes=[
+            VMEM((4, 36, RANK, RANK), bf16),
+            VMEM((7, QUAD, COLS), f32),
+            VMEM((n_lat, n_lon * RANK, COLS), f32),
+            VMEM((36, RANK, RANK), bf16),
+            VMEM((n_lat * n_lon, RANK, RANK), f32),
             VMEM((n_lat // 2, n_lon // 2, RANK, RANK), bf16),
-            pltpu.SemaphoreType.DMA((1,)),
+            VMEM((4, RANK, RANK), f32),
+            pltpu.SemaphoreType.DMA((19,)),
         ],
         compiler_params=params(),
         cost_estimate=LOW,
@@ -437,19 +490,35 @@
     flags, place8, weights, left_y, right_y, partial, basis, before, out, *scratch
 ):
     parity = lat_parity()
-    far = partial[...] + window_sum(
-        flags, weights, ((4 * parity, ((left_y, PTS), None, (right_y, PTS))),)
-    )
-    acc = scratch[6]
-
-    def fill(_):
+    near_refs, (weights_v, cells, basis_v, sems) = scratch[:-4], scratch[-4:]
+    at = PTS + QUAD
+    copies = []
+    for source, target in (
+        (block(left_y, PTS, QUAD), cells.at[0]),
+        (block(right_y, PTS, QUAD), cells.at[1]),
+        (partial, cells.at[2]),
+        (weights.at[:, pl.ds(24 * parity, 12)], weights_v),
+        (basis, basis_v),
+    ):
+        copy = pltpu.make_async_copy(source, target, sems.at[len(copies)])
+        copy.start()
+        copies.append(copy)
+
+    def fill(acc, _):
+        for copy in copies:
+            copy.wait()
+        band = (4 * parity, ((cells.at[0], 0), None, (cells.at[1], 0)))
+        far = cells[2] + window_sum(flags, weights_v, (band,), 24 * parity)
         for leaf in range(4):
-            acc[leaf] += mm3(basis[leaf], far[leaf * RANK : (leaf + 1) * RANK, :], (0, 0))
-
-    base = PTS + QUAD + 8 - 8 * parity
-    slots = [(left_y[:PTS, :], left_y, base + 4), (right_y[:PTS, :], right_y, base)]
+            acc[leaf] += mm3(basis_v[leaf], far[leaf * RANK : (leaf + 1) * RANK, :], (0, 0))
+
+    base = 8 - 8 * parity
+    slots = [
+        (block(left_y, 0, PTS), block(left_y, at, 16), base + 4),
+        (block(right_y, 0, PTS), block(right_y, at, 16), base),
+    ]
     pairs = [(s, 3 * parity - 1, 3 * s - 1, parity, s) for s in range(2)]
-    near_blocks(flags, place8, slots, pairs, before, out, scratch, fill)
+    near_blocks(flags, place8, slots, pairs, before, out, near_refs, fill)
 
 
 def local(
@@ -486,33 +555,30 @@
         flat, basis, transfer, positions.reshape(4, 2, PTS)
     )
     dev_pair = lax.ppermute(dev, "lon", partner)
+    from_c = lax.ppermute(to_c, "lat", in_chip)
+    from_y = lax.ppermute(to_y, "lat", across)
+
+    pair = jnp.concatenate([dev, dev_pair], 0)
+    moved = [
+        lax.ppermute(pair, "lon", [(i, (i + step) % n_lon) for i in range(n_lon)])
+        for step in range(2, n_lon, 2)
+    ]
+    a_right, a_left, *moved = barrier((a_right, a_left, *moved))
     left = lax.ppermute(a_right, "lon", to_right)
     right = lax.ppermute(a_left, "lon", to_left)
-    from_c = lax.ppermute(to_c, "lat", in_chip)
-    from_y = lax.ppermute(to_y, "lat", across)
-
-    dev_a = jnp.concatenate([dev, dev_pair], 0)
-    step = 2
-    moved = lax.ppermute(dev_a, "lon", [(i, (i + step) % n_lon) for i in range(n_lon)])
-    moved, from_c, place8 = barrier((moved, from_c, place8))
+    dev_a = jnp.concatenate([pair, *moved], 0)
+    dev_a, from_c, place8 = barrier((dev_a, from_c, place8))
+    dev_b = lax.ppermute(dev_a, "lat", across_two)
     (acc,) = near(own_kernel, "own", 4, 16, (flags, place8, flat, a_right), chained=False)
-    from_y, dev_a, acc = barrier((from_y, dev_a, acc))
-    dev_a = jnp.concatenate([dev_a, moved], 0)
-    while 2 * step < n_lon:
-        step *= 2
-        moved = lax.ppermute(dev_a, "lon", [(i, (i + step) % n_lon) for i in range(n_lon)])
-        dev_a = jnp.concatenate([dev_a, moved], 0)
+    from_y, acc = barrier((from_y, acc))
     (acc,) = near(lat_kernel, "lat", 4, 8, (flags, place8, from_y, from_c, acc))
-    dev_a, acc = barrier((dev_a, acc))
-    dev_b = lax.ppermute(dev_a, "lat", across_two)
-    left, right, dev_b, b_right, b_left, acc = barrier(
-        (left, right, dev_b, b_right, b_left, acc)
-    )
+    dev_b, acc = barrier((dev_b, acc))
+    left, right, b_right, b_left, acc = barrier((left, right, b_right, b_left, acc))
     left_b = lax.ppermute(b_right, "lon", to_right)
     right_b = lax.ppermute(b_left, "lon", to_left)
     left_y = lax.ppermute(left, "lat", across)
     right_y = lax.ppermute(right, "lat", across)
-    to_c = jnp.concatenate([left[PTS:], right[PTS:], dev_a, dev_b], 0)
+    to_c = jnp.concatenate([left, right, dev_a, dev_b], 0)
     c_ends = lax.ppermute(to_c, "lat", in_chip)
     (acc,) = near(lon_kernel, "lon", 2, 4, (flags, place8, left, right, acc))
     c_ends, acc = barrier((c_ends, acc))
@@ -544,6 +610,12 @@
         2,
         (flags, place8, weights, left_y, right_y, partial, basis, acc),
         cost=LOW,
+        scratch=[
+            VMEM((4, 12, RANK, RANK), bf16),
+            VMEM((3, QUAD, COLS), f32),
+            VMEM((4, RANK, PTS), f32),
+            pltpu.SemaphoreType.DMA((5,)),
+        ],
     )
     left_b, right_b, acc = barrier((left_b, right_b, acc))
     left_c = lax.ppermute(left_b, "lat", in_chip)

time: 114 us -> 112 us (0.982)
  the two profiles are of different devices: /device:TPU:1 before, /device:TPU:9 now
where the time goes in v3:
time: 112 us; the launch traced here: 111 us
  Pallas kernels  59.8 us (53%)
  waiting for transfers between devices  22.3 us (20%)
  starting transfers between devices  21 us (19%)
  local copies, waits for them, and re-layouts  4.11 us (4%)
  other arithmetic  3.42 us (3%)
    pallas_call x5, Pallas kernels, near(): pl.pallas_call(kernel, in_specs=[scalars, whole] + [hbm] * (len(operands)...  47 us
    pallas_call x1, Pallas kernels, far_field(): pl.pallas_call(functools.partial(far_kernel, n_lat, n_lon), in_specs=[sca...  7.08 us
    ppermute x3, waiting for transfers between devices, local(): lax.ppermute(pair, 'lon', [(i, (i + step) % n_lon) for i in range(n_lon)])  6.19 us
    pallas_call x1, Pallas kernels, coefficients(): pl.pallas_call(coef_kernel, in_specs=[hbm, hbm, whole, whole], out_specs=...  5.72 us
    ppermute x1, starting transfers between devices, local(): from_y = lax.ppermute(to_y, 'lat', across)  4.71 us
    ppermute x1, waiting for transfers between devices, local(): left = lax.ppermute(a_right, 'lon', to_right)  4.16 us
    ppermute x3, starting transfers between devices, local(): lax.ppermute(pair, 'lon', [(i, (i + step) % n_lon) for i in range(n_lon)])  3.77 us
    concatenate x1, other arithmetic, local(): to_c = jnp.concatenate([left, right, dev_a, dev_b], 0)  3.42 us
  transfers between devices with their start and end apart: 16, of which 9 were waited for; matrix products, arithmetic and copies ran while one was open for 4% of the time, Pallas kernels for 41%

profile of v3, /device:TPU:9, one launch (start us, length us, event | category | flops | bytes accessed | tf_op | source)
XLA Modules:
  0.0 111.0 jit_solution(14413364975469832546)
XLA Ops:
  0.0 5.7 %coefs.1 = (f32[784,256]{1,0:T(8,128)}, f32[784,256]{1,0:T(8,128)}, f32[512,256]{1,0:T(8,128)}, f32[512,256]{1,0:T(8,128)}, f32[1296,256]{1,0:T(8,128)}, /*index...) custom-call(f32[4,512,256]{2,1,0:T(8,128)} %bitcast.25, f32[4,64,512]{2,1,0:T(8,128)} %bitcast.15, ...), custom_call_target="tpu_custom_call" | custom-call | flops 20000000000 | bytes 4000000 | tf_op jit(solution)/shard_map/coefs/pallas_call | solution.py:130
  5.7 0.7 collective-permute-start.4
  6.5 1.2 %collective-permute-start = (f32[64,256]{1,0:T(8,128)}, f32[64,256]{1,0:T(8,128)S(1)}, u32[]{:S(2)}, u32[]{:S(2)}) collective-permute-start(f32[64,256]{1,0:T(8,128)} %get-tuple-element.38), channel_id=1, source_target_pairs={{0,1},{1,0},{2,3},{3,2},{4,5},{5,4},{6,7},{7,6},{8,9},{9,8},{10,11... | collective-permute-start | bytes 196616 | tf_op jit(solution)/shard_map/ppermute | solution.py:557
  7.7 1.5 %constant_dynamic-update-slice_fusion.1 = (f32[128,256]{1,0:T(8,128)S(1)}, f32[512,256]{1,0:T(8,128)}) fusion(f32[64,256]{1,0:T(8,128)} %get-tuple-element.38), kind=kLoop, calls=%fused_computation.2 | loop fusion | bytes 196608
  9.2 1.1 %collective-permute-done = f32[64,256]{1,0:T(8,128)S(1)} collective-permute-done((f32[64,256]{1,0:T(8,128)}, f32[64,256]{1,0:T(8,128)S(1)}, u32[]{:S(2)}, u32[]{:S(2)}) %collective-permute-start) | collective-permute-done | bytes 65568 | tf_op jit(solution)/shard_map/ppermute | solution.py:557
  11.0 1.3 %collective-permute-start.1 = (f32[128,256]{1,0:T(8,128)S(1)}, f32[128,256]{1,0:T(8,128)S(1)}, u32[]{:S(2)}, u32[]{:S(2)}) collective-permute-start(f32[128,256]{1,0:T(8,128)S(1)} %get-tuple-element.71), channel_id=1, source_target_pairs={{0,2},{1,3},{2,4},{3,5},{4,6},{5,7},{6,0},{7,1},{8,10},{9,11},{10,... | collective-permute-start | bytes 393224 | tf_op jit(solution)/shard_map/ppermute | solution.py:563
  12.3 1.0 collective-permute-start.2
  13.3 1.5 %collective-permute-start.3 = (f32[128,256]{1,0:T(8,128)S(1)}, f32[128,256]{1,0:T(8,128)S(1)}, u32[]{:S(2)}, u32[]{:S(2)}) collective-permute-start(f32[128,256]{1,0:T(8,128)S(1)} %get-tuple-element.71), channel_id=1, source_target_pairs={{0,6},{1,7},{2,0},{3,1},{4,2},{5,3},{6,4},{7,5},{8,14},{9,15},{10,... | collective-permute-start | bytes 393224 | tf_op jit(solution)/shard_map/ppermute | solution.py:563
  14.8 4.7 %collective-permute-start.8 = (f32[1296,256]{1,0:T(8,128)}, f32[1296,256]{1,0:T(8,128)}, u32[]{:S(2)}, u32[]{:S(2)}) collective-permute-start(f32[1296,256]{1,0:T(8,128)} %get-tuple-element.52), channel_id=1, source_target_pairs={{8,16},{16,8},{9,17},{17,9},{10,18},{18,10},{11,19},{19,11},{12,20... | collective-permute-start | bytes 3981320 | tf_op jit(solution)/shard_map/ppermute | solution.py:559
  19.5 3.2 %collective-permute-done.2 = f32[128,256]{1,0:T(8,128)S(1)} collective-permute-done((f32[128,256]{1,0:T(8,128)S(1)}, f32[128,256]{1,0:T(8,128)S(1)}, u32[]{:S(2)}, u32[]{:S(2)}) %collective-permute-start.2) | collective-permute-done | bytes 131104 | tf_op jit(solution)/shard_map/ppermute | solution.py:563
  22.7 3.0 %collective-permute-done.3 = f32[128,256]{1,0:T(8,128)S(1)} collective-permute-done((f32[128,256]{1,0:T(8,128)S(1)}, f32[128,256]{1,0:T(8,128)S(1)}, u32[]{:S(2)}, u32[]{:S(2)}) %collective-permute-start.3) | collective-permute-done | bytes 131104 | tf_op jit(solution)/shard_map/ppermute | solution.py:563
  25.7 1.2 %collective-permute-start.5 = (f32[784,256]{1,0:T(8,128)}, f32[784,256]{1,0:T(8,128)}, u32[]{:S(2)}, u32[]{:S(2)}) collective-permute-start(f32[784,256]{1,0:T(8,128)} %get-tuple-element.47.msg.own), channel_id=1, source_target_pairs={{0,1},{1,2},{2,3},{3,4},{4,5},{5,6},{6,7},{7,0},{8,9},{9,10},{10,1... | collective-permute-start | bytes 2408456 | tf_op jit(solution)/shard_map/ppermute | solution.py:567
  26.9 1.1 %collective-permute-start.6 = (f32[784,256]{1,0:T(8,128)}, f32[784,256]{1,0:T(8,128)}, u32[]{:S(2)}, u32[]{:S(2)}) collective-permute-start(f32[784,256]{1,0:T(8,128)} %get-tuple-element.48), channel_id=1, source_target_pairs={{0,7},{1,0},{2,1},{3,2},{4,3},{5,4},{6,5},{7,6},{8,15},{9,8},{10,9... | collective-permute-start | bytes 2408456 | tf_op jit(solution)/shard_map/ppermute | solution.py:568
  28.0 0.7 constant_dynamic-update-slice_fusion.4
  28.7 0.7 constant_dynamic-update-slice_fusion.3
  29.3 0.7 constant_dynamic-update-slice_fusion.2.dev_a
  30.0 15.1 %own.1.before = f32[4,512,256]{2,1,0:T(8,128)} custom-call(s32[4,9]{1,0:T(4,128)} %bitcast.19, f32[4,8,512]{2,1,0:T(8,128)} %get-tuple-element.46.place8, f32[4,512,256]{2,1,0:T(8,128)} %bitcast.26, f32[784,256]{1,0:T(8,128)} %get-tuple-element.47.msg.own), custom_call_target="tpu_custom_call" | custom-call | flops 20000000000 | bytes 4000000 | tf_op jit(solution)/shard_map/own/pallas_call | solution.py:334
  45.2 9.4 %lat.1.before = f32[4,512,256]{2,1,0:T(8,128)} custom-call(s32[4,9]{1,0:T(4,128)} %bitcast.20, f32[4,8,512]{2,1,0:T(8,128)} %get-tuple-element.46.place8, f32[1296,256]{1,0:T(8,128)} %collective-permute-done.8.from_y, f32[1296,256]{1,0:T(8,128)} %collective-permute-done.4.from_c, f32[4,512,256]{2,1,0:T(8,128)} %own.1.before), custom_call_target="tpu_custom_call", output_to_operand_aliasing={{}: (4, {})} | custom-call | flops 20000000000 | bytes 4000000 | tf_op jit(solution)/shard_map/lat/pallas_call | solution.py:334
  54.7 2.4 %collective-permute-done.7.dev_b = f32[512,256]{1,0:T(8,128)} collective-permute-done((f32[512,256]{1,0:T(8,128)}, f32[512,256]{1,0:T(8,128)}, u32[]{:S(2)}, u32[]{:S(2)}) %collective-permute-start.7) | collective-permute-done | bytes 524320 | tf_op jit(solution)/shard_map/ppermute | solution.py:571
  57.0 4.2 %collective-permute-done.5.left.a_left = f32[784,256]{1,0:T(8,128)} collective-permute-done((f32[784,256]{1,0:T(8,128)}, f32[784,256]{1,0:T(8,128)}, u32[]{:S(2)}, u32[]{:S(2)}) %collective-permute-start.5) | collective-permute-done | bytes 802848 | tf_op jit(solution)/shard_map/ppermute | solution.py:567
  61.2 2.7 %collective-permute-done.6.right.a_right = f32[784,256]{1,0:T(8,128)} collective-permute-done((f32[784,256]{1,0:T(8,128)}, f32[784,256]{1,0:T(8,128)}, u32[]{:S(2)}, u32[]{:S(2)}) %collective-permute-start.6) | collective-permute-done | bytes 802848 | tf_op jit(solution)/shard_map/ppermute | solution.py:568
  63.9 3.4 %pad_maximum_fusion = f32[2592,256]{1,0:T(8,128)} fusion(f32[512,256]{1,0:T(8,128)} %collective-permute-done.7.dev_b, f32[512,256]{1,0:T(8,128)} %constant_dynamic-update-slice_fusion.2.dev_a, f32[784,256]{1,0:T(8,128)} %collective-permute-done.6.right.a_right, f32[784,256]{1,0:T(8,128)} %collective-permute-done.5.left.a_left), kind=kLoop, calls=%fused_computation | loop fusion | flops 1990656 | bytes 5308416 | tf_op jit(solution)/shard_map/concatenate | solution.py:581
  67.8 3.1 %collective-permute-start.11 = (f32[784,256]{1,0:T(8,128)}, f32[784,256]{1,0:T(8,128)}, u32[]{:S(2)}, u32[]{:S(2)}) collective-permute-start(f32[784,256]{1,0:T(8,128)} %collective-permute-done.5.left.a_left), channel_id=1, source_target_pairs={{8,16},{16,8},{9,17},{17,9},{10,18},{18,10},{11,19},{19,11},{12,20... | collective-permute-start | bytes 2408456 | tf_op jit(solution)/shard_map/ppermute | solution.py:579
  71.0 2.4 %collective-permute-start.12 = (f32[784,256]{1,0:T(8,128)}, f32[784,256]{1,0:T(8,128)}, u32[]{:S(2)}, u32[]{:S(2)}) collective-permute-start(f32[784,256]{1,0:T(8,128)} %collective-permute-done.6.right.a_right), channel_id=1, source_target_pairs={{8,16},{16,8},{9,17},{17,9},{10,18},{18,10},{11,19},{19,11},{12,20... | collective-permute-start | bytes 2408456 | tf_op jit(solution)/shard_map/ppermute | solution.py:580
  73.5 1.5 %collective-permute-start.9 = (f32[512,256]{1,0:T(8,128)}, f32[512,256]{1,0:T(8,128)}, u32[]{:S(2)}, u32[]{:S(2)}) collective-permute-start(f32[512,256]{1,0:T(8,128)} %get-tuple-element.59), channel_id=1, source_target_pairs={{0,1},{1,2},{2,3},{3,4},{4,5},{5,6},{6,7},{7,0},{8,9},{9,10},{10,1... | collective-permute-start | bytes 1572872 | tf_op jit(solution)/shard_map/ppermute | solution.py:577
  74.9 5.2 %lon.1.before = f32[4,512,256]{2,1,0:T(8,128)} custom-call(s32[4,9]{1,0:T(4,128)} %bitcast.21, f32[4,8,512]{2,1,0:T(8,128)} %get-tuple-element.46.place8, f32[784,256]{1,0:T(8,128)} %collective-permute-done.5.left.a_left, f32[784,256]{1,0:T(8,128)} %collective-permute-done.6.right.a_right, f32[4,512,256]{2,1,0:T(8,128)} %lat.1.before), custom_call_target="tpu_custom_call", output_to_operand_aliasing={{}: (4, {})} | custom-call | flops 20000000000 | bytes 4000000 | tf_op jit(solution)/shard_map/lon/pallas_call | solution.py:334
  80.2 7.1 %far.1.partial = f32[256,256]{1,0:T(8,128)} custom-call(s32[4,9]{1,0:T(4,128)} %bitcast.22, bf16[4,36,64,64]{3,2,1,0:T(8,128)(2,1)} %bitcast.11, f32[784,256]{1,0:T(8,128)} %get-tuple-element.47.msg.own, f32[784,256]{1,0:T(8,128)} %collective-permute-done.5.left.a_left, f32[784,256]{1,0:T(8,128)} %collective-permute-done.6.right.a_right, ...), custom_call_target="tpu_custom_call" | custom-call | flops 1000 | bytes 1000 | tf_op jit(solution)/shard_map/far/pallas_call | solution.py:468
  87.3 3.2 %collective-permute-done.12.right_y = f32[784,256]{1,0:T(8,128)} collective-permute-done((f32[784,256]{1,0:T(8,128)}, f32[784,256]{1,0:T(8,128)}, u32[]{:S(2)}, u32[]{:S(2)}) %collective-permute-start.12) | collective-permute-done | bytes 802848 | tf_op jit(solution)/shard_map/ppermute | solution.py:580
  90.5 9.2 %down.1.before = f32[4,512,256]{2,1,0:T(8,128)} custom-call(s32[4,9]{1,0:T(4,128)} %bitcast.23, f32[4,8,512]{2,1,0:T(8,128)} %get-tuple-element.46.place8, bf16[4,36,64,64]{3,2,1,0:T(8,128)(2,1)} %bitcast.12, f32[784,256]{1,0:T(8,128)} %collective-permute-done.11.left_y, f32[784,256]{1,0:T(8,128)} %collective-permute-done.12.right_y, ...), custom_call_target="tpu_custom_call", output_to_operand_aliasing={{}: (7, {})} | custom-call | flops 1000 | bytes 1000 | tf_op jit(solution)/shard_map/down/pallas_call | solution.py:334
  100.3 1.7 %collective-permute-done.14.left_c = f32[512,256]{1,0:T(8,128)} collective-permute-done((f32[512,256]{1,0:T(8,128)}, f32[512,256]{1,0:T(8,128)}, u32[]{:S(2)}, u32[]{:S(2)}) %collective-permute-start.14) | collective-permute-done | bytes 524320 | tf_op jit(solution)/shard_map/ppermute | solution.py:621
  102.0 0.7 collective-permute-done.15.right_c
  102.8 8.0 %last.1 = f32[4,512,256]{2,1,0:T(8,128)} custom-call(s32[4,9]{1,0:T(4,128)} %bitcast.24, f32[4,8,512]{2,1,0:T(8,128)} %get-tuple-element.46.place8, f32[784,256]{1,0:T(8,128)} %collective-permute-done.5.left.a_left, f32[784,256]{1,0:T(8,128)} %collective-permute-done.6.right.a_right, ...), custom_call_target="tpu_custom_call", output_to_operand_aliasing={{}: (9, {})} | custom-call | flops 20000000000 | bytes 4000000 | tf_op jit(solution)/shard_map/last/pallas_call | solution.py:334
  (13 shorter events, 1.8 us)
Async XLA Ops:
  5.7 24.3 %collective-permute-start.4 = (f32[1296,256]{1,0:T(8,128)}, f32[1296,256]{1,0:T(8,128)}, u32[]{:S(2)}, u32[]{:S(2)}) collective-permute-start(f32[1296,256]{1,0:T(8,128)} %get-tuple-element.44), channel_id=1, source_target_pairs={{0,8},{8,0},{16,24},{24,16},{1,9},{9,1},{17,25},{25,17},{2,10},{10... | collective-permute-start | bytes 3981320 | tf_op jit(solution)/shard_map/ppermute | solution.py:558
  6.5 3.9 %collective-permute-start = (f32[64,256]{1,0:T(8,128)}, f32[64,256]{1,0:T(8,128)S(1)}, u32[]{:S(2)}, u32[]{:S(2)}) collective-permute-start(f32[64,256]{1,0:T(8,128)} %get-tuple-element.38), channel_id=1, source_target_pairs={{0,1},{1,0},{2,3},{3,2},{4,5},{5,4},{6,7},{7,6},{8,9},{9,8},{10,11... | collective-permute-start | bytes 196616 | tf_op jit(solution)/shard_map/ppermute | solution.py:557
  11.0 8.5 %collective-permute-start.1 = (f32[128,256]{1,0:T(8,128)S(1)}, f32[128,256]{1,0:T(8,128)S(1)}, u32[]{:S(2)}, u32[]{:S(2)}) collective-permute-start(f32[128,256]{1,0:T(8,128)S(1)} %get-tuple-element.71), channel_id=1, source_target_pairs={{0,2},{1,3},{2,4},{3,5},{4,6},{5,7},{6,0},{7,1},{8,10},{9,11},{10,... | collective-permute-start | bytes 393224 | tf_op jit(solution)/shard_map/ppermute | solution.py:563
  12.3 10.4 %collective-permute-start.2 = (f32[128,256]{1,0:T(8,128)S(1)}, f32[128,256]{1,0:T(8,128)S(1)}, u32[]{:S(2)}, u32[]{:S(2)}) collective-permute-start(f32[128,256]{1,0:T(8,128)S(1)} %get-tuple-element.71), channel_id=1, source_target_pairs={{0,4},{1,5},{2,6},{3,7},{4,0},{5,1},{6,2},{7,3},{8,12},{9,13},{10,... | collective-permute-start | bytes 393224 | tf_op jit(solution)/shard_map/ppermute | solution.py:563
  13.3 12.4 %collective-permute-start.3 = (f32[128,256]{1,0:T(8,128)S(1)}, f32[128,256]{1,0:T(8,128)S(1)}, u32[]{:S(2)}, u32[]{:S(2)}) collective-permute-start(f32[128,256]{1,0:T(8,128)S(1)} %get-tuple-element.71), channel_id=1, source_target_pairs={{0,6},{1,7},{2,0},{3,1},{4,2},{5,3},{6,4},{7,5},{8,14},{9,15},{10,... | collective-permute-start | bytes 393224 | tf_op jit(solution)/shard_map/ppermute | solution.py:563
  14.8 30.4 %collective-permute-start.8 = (f32[1296,256]{1,0:T(8,128)}, f32[1296,256]{1,0:T(8,128)}, u32[]{:S(2)}, u32[]{:S(2)}) collective-permute-start(f32[1296,256]{1,0:T(8,128)} %get-tuple-element.52), channel_id=1, source_target_pairs={{8,16},{16,8},{9,17},{17,9},{10,18},{18,10},{11,19},{19,11},{12,20... | collective-permute-start | bytes 3981320 | tf_op jit(solution)/shard_map/ppermute | solution.py:559
  25.7 35.5 %collective-permute-start.5 = (f32[784,256]{1,0:T(8,128)}, f32[784,256]{1,0:T(8,128)}, u32[]{:S(2)}, u32[]{:S(2)}) collective-permute-start(f32[784,256]{1,0:T(8,128)} %get-tuple-element.47.msg.own), channel_id=1, source_target_pairs={{0,1},{1,2},{2,3},{3,4},{4,5},{5,6},{6,7},{7,0},{8,9},{9,10},{10,1... | collective-permute-start | bytes 2408456 | tf_op jit(solution)/shard_map/ppermute | solution.py:567
  26.9 37.0 %collective-permute-start.6 = (f32[784,256]{1,0:T(8,128)}, f32[784,256]{1,0:T(8,128)}, u32[]{:S(2)}, u32[]{:S(2)}) collective-permute-start(f32[784,256]{1,0:T(8,128)} %get-tuple-element.48), channel_id=1, source_target_pairs={{0,7},{1,0},{2,1},{3,2},{4,3},{5,4},{6,5},{7,6},{8,15},{9,8},{10,9... | collective-permute-start | bytes 2408456 | tf_op jit(solution)/shard_map/ppermute | solution.py:568
  45.1 11.9 %collective-permute-start.7 = (f32[512,256]{1,0:T(8,128)}, f32[512,256]{1,0:T(8,128)}, u32[]{:S(2)}, u32[]{:S(2)}) collective-permute-start(f32[512,256]{1,0:T(8,128)} %constant_dynamic-update-slice_fusion.2.dev_a), channel_id=1, source_target_pairs={{0,16},{8,24},{16,0},{24,8},{1,17},{9,25},{17,1},{25,9},{2,18},{10... | collective-permute-start | bytes 1572872 | tf_op jit(solution)/shard_map/ppermute | solution.py:571
  67.3 12.8 %collective-permute-start.13 = (f32[2592,256]{1,0:T(8,128)}, f32[2592,256]{1,0:T(8,128)}, u32[]{:S(2)}, u32[]{:S(2)}) collective-permute-start(f32[2592,256]{1,0:T(8,128)} %pad_maximum_fusion), channel_id=1, source_target_pairs={{0,8},{8,0},{16,24},{24,16},{1,9},{9,1},{17,25},{25,17},{2,10},{10... | collective-permute-start | bytes 7962632 | tf_op jit(solution)/shard_map/ppermute | solution.py:582
  67.8 19.4 %collective-permute-start.11 = (f32[784,256]{1,0:T(8,128)}, f32[784,256]{1,0:T(8,128)}, u32[]{:S(2)}, u32[]{:S(2)}) collective-permute-start(f32[784,256]{1,0:T(8,128)} %collective-permute-done.5.left.a_left), channel_id=1, source_target_pairs={{8,16},{16,8},{9,17},{17,9},{10,18},{18,10},{11,19},{19,11},{12,20... | collective-permute-start | bytes 2408456 | tf_op jit(solution)/shard_map/ppermute | solution.py:579
  71.0 19.5 %collective-permute-start.12 = (f32[784,256]{1,0:T(8,128)}, f32[784,256]{1,0:T(8,128)}, u32[]{:S(2)}, u32[]{:S(2)}) collective-permute-start(f32[784,256]{1,0:T(8,128)} %collective-permute-done.6.right.a_right), channel_id=1, source_target_pairs={{8,16},{16,8},{9,17},{17,9},{10,18},{18,10},{11,19},{19,11},{12,20... | collective-permute-start | bytes 2408456 | tf_op jit(solution)/shard_map/ppermute | solution.py:580
  73.4 26.3 %collective-permute-start.10 = (f32[512,256]{1,0:T(8,128)}, f32[512,256]{1,0:T(8,128)}, u32[]{:S(2)}, u32[]{:S(2)}) collective-permute-start(f32[512,256]{1,0:T(8,128)} %get-tuple-element.60), channel_id=1, source_target_pairs={{0,7},{1,0},{2,1},{3,2},{4,3},{5,4},{6,5},{7,6},{8,15},{9,8},{10,9... | collective-permute-start | bytes 1572872 | tf_op jit(solution)/shard_map/ppermute | solution.py:578
  73.5 26.3 %collective-permute-start.9 = (f32[512,256]{1,0:T(8,128)}, f32[512,256]{1,0:T(8,128)}, u32[]{:S(2)}, u32[]{:S(2)}) collective-permute-start(f32[512,256]{1,0:T(8,128)} %get-tuple-element.59), channel_id=1, source_target_pairs={{0,1},{1,2},{2,3},{3,4},{4,5},{5,6},{6,7},{7,0},{8,9},{9,10},{10,1... | collective-permute-start | bytes 1572872 | tf_op jit(solution)/shard_map/ppermute | solution.py:577
  99.7 2.3 %collective-permute-start.14 = (f32[512,256]{1,0:T(8,128)}, f32[512,256]{1,0:T(8,128)}, u32[]{:S(2)}, u32[]{:S(2)}) collective-permute-start(f32[512,256]{1,0:T(8,128)} %collective-permute-done.9.left), channel_id=1, source_target_pairs={{0,8},{8,0},{16,24},{24,16},{1,9},{9,1},{17,25},{25,17},{2,10},{10... | collective-permute-start | bytes 1572872 | tf_op jit(solution)/shard_map/ppermute | solution.py:621
  99.8 3.0 %collective-permute-start.15 = (f32[512,256]{1,0:T(8,128)}, f32[512,256]{1,0:T(8,128)}, u32[]{:S(2)}, u32[]{:S(2)}) collective-permute-start(f32[512,256]{1,0:T(8,128)} %collective-permute-done.10.right), channel_id=1, source_target_pairs={{0,8},{8,0},{16,24},{24,16},{1,9},{9,1},{17,25},{25,17},{2,10},{10... | collective-permute-start | bytes 1572872 | tf_op jit(solution)/shard_map/ppermute | solution.py:622

commit v4 on v3

--- a/solution.py
+++ b/solution.py
@@ -374,7 +374,7 @@
 
 
 def far_kernel(
-    n_lat, n_lon, flags, weights, own, left, right, from_y, from_c, dev_a, dev_b, c_ends,
+    n_lat, n_lon, flags, weights, own, left, right, from_y, from_c, devices, c_ends,
     dev_w, dev_t, group_w, leaf_t, out, weights_v, cells, rows_dev, dev_w_v, dev_t_v,
     group_row_w, leaf_t_v, sems,
 ):
@@ -384,15 +384,12 @@
     side = lax.rem(lon, 2)
     group_row, group_col = lat // 2, lon // 2
     n_gcol = n_lon // 2
-    size = n_lon * RANK
-    ends = 2 * (PTS + MSG)
+    size = 2 * n_lon * RANK
     copies = []
     for source, target in (
         (dev_w, dev_w_v),
-        (dev_a, rows_dev.at[0]),
-        (block(c_ends, ends, size), rows_dev.at[1]),
-        (dev_b, rows_dev.at[2]),
-        (block(c_ends, ends + size, size), rows_dev.at[3]),
+        (devices, rows_dev.at[0]),
+        (block(c_ends, 2 * (PTS + MSG), size), rows_dev.at[1]),
         (group_w.at[group_row, group_col], group_row_w),
         (dev_t, dev_t_v),
         (leaf_t, leaf_t_v),
@@ -411,13 +408,13 @@
         copy = pltpu.make_async_copy(source, target, sems.at[len(copies)])
         copy.start()
         copies.append(copy)
-    for copy in copies[:5]:
+    for copy in copies[:3]:
         copy.wait()
 
     def device_coef(k, back, col_side):
         which = jnp.where(side == col_side, 0, 1)
-        start = pl.multiple_of((2 * back + which) * RANK, RANK)
-        return rows_dev[k, pl.ds(start, RANK), :]
+        start = pl.multiple_of((4 * back + 2 * (k // 2) + which) * RANK, RANK)
+        return rows_dev[k % 2, pl.ds(start, RANK), :]
 
     total = jnp.zeros((RANK, COLS), f32)
     for k in range(n_lat):
@@ -429,7 +426,7 @@
             scale = jnp.where(drop, 0.0, 1.0)
             coef = device_coef(k, (1 - v // 2) % n_gcol, v % 2)
             total = total + scale * mm2(dev_w_v[6 * u + v], coef)
-    for copy in copies[5:8]:
+    for copy in copies[3:6]:
         copy.wait()
 
     def group_step(step, field):
@@ -448,7 +445,7 @@
 
     field = lax.fori_loop(2, n_gcol - 1, group_step, jnp.zeros((RANK, COLS), f32))
     total = total + mm3(dev_t_v[lat * n_lon + lon], field)
-    for copy in copies[8:]:
+    for copy in copies[6:]:
         copy.wait()
     far = window_sum(
         flags,
@@ -467,18 +464,18 @@
 def far_field(n_lat, n_lon, operands):
     return pl.pallas_call(
         functools.partial(far_kernel, n_lat, n_lon),
-        in_specs=[scalars] + [hbm] * 13,
+        in_specs=[scalars] + [hbm] * 12,
         out_specs=whole,
         out_shape=shape(QUAD, COLS),
         scratch_shapes=[
             VMEM((4, 36, RANK, RANK), bf16),
             VMEM((7, QUAD, COLS), f32),
-            VMEM((n_lat, n_lon * RANK, COLS), f32),
+            VMEM((2, 2 * n_lon * RANK, COLS), f32),
             VMEM((36, RANK, RANK), bf16),
             VMEM((n_lat * n_lon, RANK, RANK), f32),
             VMEM((n_lat // 2, n_lon // 2, RANK, RANK), bf16),
             VMEM((4, RANK, RANK), f32),
-            pltpu.SemaphoreType.DMA((19,)),
+            pltpu.SemaphoreType.DMA((17,)),
         ],
         compiler_params=params(),
         cost_estimate=LOW,
@@ -558,27 +555,28 @@
     from_c = lax.ppermute(to_c, "lat", in_chip)
     from_y = lax.ppermute(to_y, "lat", across)
 
+    left = lax.ppermute(a_right, "lon", to_right)
+    right = lax.ppermute(a_left, "lon", to_left)
     pair = jnp.concatenate([dev, dev_pair], 0)
+    pair_two = lax.ppermute(pair, "lat", across_two)
+    from_c, place8 = barrier((from_c, place8))
+    (acc,) = near(own_kernel, "own", 4, 16, (flags, place8, flat, a_right), chained=False)
+    from_y, pair_two, acc = barrier((from_y, pair_two, acc))
+    quad = jnp.concatenate([pair, pair_two], 0)
     moved = [
-        lax.ppermute(pair, "lon", [(i, (i + step) % n_lon) for i in range(n_lon)])
+        lax.ppermute(quad, "lon", [(i, (i + step) % n_lon) for i in range(n_lon)])
         for step in range(2, n_lon, 2)
     ]
-    a_right, a_left, *moved = barrier((a_right, a_left, *moved))
-    left = lax.ppermute(a_right, "lon", to_right)
-    right = lax.ppermute(a_left, "lon", to_left)
-    dev_a = jnp.concatenate([pair, *moved], 0)
-    dev_a, from_c, place8 = barrier((dev_a, from_c, place8))
-    dev_b = lax.ppermute(dev_a, "lat", across_two)
-    (acc,) = near(own_kernel, "own", 4, 16, (flags, place8, flat, a_right), chained=False)
-    from_y, acc = barrier((from_y, acc))
     (acc,) = near(lat_kernel, "lat", 4, 8, (flags, place8, from_y, from_c, acc))
-    dev_b, acc = barrier((dev_b, acc))
-    left, right, b_right, b_left, acc = barrier((left, right, b_right, b_left, acc))
+    devices = jnp.concatenate([quad, *moved], 0)
+    left, right, b_right, b_left, devices, acc = barrier(
+        (left, right, b_right, b_left, devices, acc)
+    )
     left_b = lax.ppermute(b_right, "lon", to_right)
     right_b = lax.ppermute(b_left, "lon", to_left)
     left_y = lax.ppermute(left, "lat", across)
     right_y = lax.ppermute(right, "lat", across)
-    to_c = jnp.concatenate([left, right, dev_a, dev_b], 0)
+    to_c = jnp.concatenate([left, right, devices], 0)
     c_ends = lax.ppermute(to_c, "lat", in_chip)
     (acc,) = near(lon_kernel, "lon", 2, 4, (flags, place8, left, right, acc))
     c_ends, acc = barrier((c_ends, acc))
@@ -593,8 +591,7 @@
             right,
             from_y,
             from_c,
-            dev_a,
-            dev_b,
+            devices,
             c_ends,
             device_coupling.reshape(36, RANK, RANK),
             device_transfer.reshape(n_lat * n_lon, RANK, RANK),

time: 112 us -> 109 us (0.973)
  the two profiles are of different devices: /device:TPU:9 before, /device:TPU:25 now
where the time goes in v4:
time: 109 us; the launch traced here: 108 us
  Pallas kernels  55.3 us (51%)
  starting transfers between devices  21.6 us (20%)
  waiting for transfers between devices  16 us (15%)
  local copies, waits for them, and re-layouts  9.53 us (9%)
  other arithmetic  4.95 us (5%)
    pallas_call x5, Pallas kernels, near(): pl.pallas_call(kernel, in_specs=[scalars, whole] + [hbm] * (len(operands)...  42.5 us
    ppermute x3, waiting for transfers between devices, local(): lax.ppermute(quad, 'lon', [(i, (i + step) % n_lon) for i in range(n_lon)])  12 us
    pallas_call x1, Pallas kernels, far_field(): pl.pallas_call(functools.partial(far_kernel, n_lat, n_lon), in_specs=[sca...  7.09 us
    unnamed x6, local copies, waits for them, and re-layouts  6.19 us
    pallas_call x1, Pallas kernels, coefficients(): pl.pallas_call(coef_kernel, in_specs=[hbm, hbm, whole, whole], out_specs=...  5.71 us
    concatenate x1, other arithmetic, local(): to_c = jnp.concatenate([left, right, devices], 0)  3.45 us
    ppermute x1, starting transfers between devices, local(): from_y = lax.ppermute(to_y, 'lat', across)  3.37 us
    ppermute x1, starting transfers between devices, local(): left_y = lax.ppermute(left, 'lat', across)  3.25 us
  transfers between devices with their start and end apart: 16, of which 4 were waited for; matrix products, arithmetic and copies ran while one was open for 10% of the time, Pallas kernels for 39%

profile of v4, /device:TPU:25, one launch (start us, length us, event | category | flops | bytes accessed | tf_op | source)
XLA Modules:
  0.0 107.8 jit_solution(10913057300510601919)
XLA Ops:
  0.0 5.7 %coefs.1 = (f32[784,256]{1,0:T(8,128)}, f32[784,256]{1,0:T(8,128)}, f32[512,256]{1,0:T(8,128)}, f32[512,256]{1,0:T(8,128)}, f32[1296,256]{1,0:T(8,128)}, /*index...) custom-call(f32[4,512,256]{2,1,0:T(8,128)} %bitcast.25, f32[4,64,512]{2,1,0:T(8,128)} %bitcast.15, ...), custom_call_target="tpu_custom_call" | custom-call | flops 20000000000 | bytes 4000000 | tf_op jit(solution)/shard_map/coefs/pallas_call | solution.py:130
  5.7 0.7 collective-permute-start
  6.5 1.2 %collective-permute-start.3 = (f32[64,256]{1,0:T(8,128)}, f32[64,256]{1,0:T(8,128)S(1)}, u32[]{:S(2)}, u32[]{:S(2)}) collective-permute-start(f32[64,256]{1,0:T(8,128)} %get-tuple-element.39), channel_id=1, source_target_pairs={{0,1},{1,0},{2,3},{3,2},{4,5},{5,4},{6,7},{7,6},{8,9},{9,8},{10,11... | collective-permute-start | bytes 196616 | tf_op jit(solution)/shard_map/ppermute | solution.py:554
  7.7 3.4 %collective-permute-start.4 = (f32[1296,256]{1,0:T(8,128)}, f32[1296,256]{1,0:T(8,128)}, u32[]{:S(2)}, u32[]{:S(2)}) collective-permute-start(f32[1296,256]{1,0:T(8,128)} %get-tuple-element.40), channel_id=1, source_target_pairs={{8,16},{16,8},{9,17},{17,9},{10,18},{18,10},{11,19},{19,11},{12,20... | collective-permute-start | bytes 3981320 | tf_op jit(solution)/shard_map/ppermute | solution.py:556
  11.1 0.3 collective-permute-start.1
  11.4 2.1 %collective-permute-start.2 = (f32[784,256]{1,0:T(8,128)}, f32[784,256]{1,0:T(8,128)}, u32[]{:S(2)}, u32[]{:S(2)}) collective-permute-start(f32[784,256]{1,0:T(8,128)} %get-tuple-element.36), channel_id=1, source_target_pairs={{0,7},{1,0},{2,1},{3,2},{4,3},{5,4},{6,5},{7,6},{8,15},{9,8},{10,9... | collective-permute-start | bytes 2408456 | tf_op jit(solution)/shard_map/ppermute | solution.py:559
  13.5 1.5 %constant_dynamic-update-slice_fusion.2 = (f32[256,256]{1,0:T(8,128)S(1)}, f32[1024,256]{1,0:T(8,128)}) fusion(f32[64,256]{1,0:T(8,128)} %get-tuple-element.39), kind=kLoop, calls=%fused_computation.4 | loop fusion | bytes 196608
  15.0 1.5 %pad_maximum_fusion.1 = f32[128,256]{1,0:T(8,128)} fusion(f32[64,256]{1,0:T(8,128)S(1)} %collective-permute-done.3, f32[64,256]{1,0:T(8,128)} %get-tuple-element.39), kind=kLoop, calls=%fused_computation.1 | loop fusion | flops 32768 | bytes 262144 | tf_op jit(solution)/shard_map/concatenate | solution.py:560
  16.5 0.6 constant_dynamic-update-slice_fusion.1
  17.1 0.7 copy-done
  17.8 11.6 %own.1.before = f32[4,512,256]{2,1,0:T(8,128)} custom-call(s32[4,9]{1,0:T(4,128)} %bitcast.19, f32[4,8,512]{2,1,0:T(8,128)} %get-tuple-element.34.place8, f32[4,512,256]{2,1,0:T(8,128)} %bitcast.26, f32[784,256]{1,0:T(8,128)} %get-tuple-element.35.msg.own), custom_call_target="tpu_custom_call" | custom-call | flops 20000000000 | bytes 4000000 | tf_op jit(solution)/shard_map/own/pallas_call | solution.py:334
  29.5 1.7 %constant_dynamic-update-slice_fusion = (f32[256,256]{1,0:T(8,128)}, f32[1024,256]{1,0:T(8,128)}) fusion(f32[256,256]{1,0:T(8,128)} %copy-done, f32[128,256]{1,0:T(8,128)} %collective-permute-done.5, f32[1024,256]{1,0:T(8,128)} %get-tuple-element.62), kind=kLoop, calls=%fused_computation.2 | loop fusion | bytes 393216 | tf_op jit(solution)/shard_map/concatenate | solution.py:565
  31.1 3.1 %collective-permute-start.7 = (f32[256,256]{1,0:T(8,128)}, f32[256,256]{1,0:T(8,128)}, u32[]{:S(2)}, u32[]{:S(2)}) collective-permute-start(f32[256,256]{1,0:T(8,128)} %get-tuple-element.59), channel_id=1, source_target_pairs={{0,4},{1,5},{2,6},{3,7},{4,0},{5,1},{6,2},{7,3},{8,12},{9,13},{10,... | collective-permute-start | bytes 786440 | tf_op jit(solution)/shard_map/ppermute | solution.py:567
  34.2 7.5 %lat.1.before = f32[4,512,256]{2,1,0:T(8,128)} custom-call(s32[4,9]{1,0:T(4,128)} %bitcast.20, f32[4,8,512]{2,1,0:T(8,128)} %get-tuple-element.34.place8, f32[1296,256]{1,0:T(8,128)} %collective-permute-done.4.from_y, f32[1296,256]{1,0:T(8,128)} %collective-permute-done.from_c, f32[4,512,256]{2,1,0:T(8,128)} %own.1.before), custom_call_target="tpu_custom_call", output_to_operand_aliasing={{}: (4, {})} | custom-call | flops 20000000000 | bytes 4000000 | tf_op jit(solution)/shard_map/lat/pallas_call | solution.py:334
  41.7 1.7 %constant_dynamic-update-slice_fusion.5 = f32[1024,256]{1,0:T(8,128)} fusion(f32[1024,256]{1,0:T(8,128)} %get-tuple-element.60, f32[256,256]{1,0:T(8,128)} %collective-permute-done.6), kind=kLoop, calls=%fused_computation.7 | loop fusion | bytes 524288
  43.4 12.0 %collective-permute-done.7 = f32[256,256]{1,0:T(8,128)} collective-permute-done((f32[256,256]{1,0:T(8,128)}, f32[256,256]{1,0:T(8,128)}, u32[]{:S(2)}, u32[]{:S(2)}) %collective-permute-start.7) | collective-permute-done | bytes 262176 | tf_op jit(solution)/shard_map/ppermute | solution.py:567
  55.4 1.7 %constant_dynamic-update-slice_fusion.4 = f32[1024,256]{1,0:T(8,128)} fusion(f32[1024,256]{1,0:T(8,128)} %constant_dynamic-update-slice_fusion.5, f32[256,256]{1,0:T(8,128)} %collective-permute-done.7), kind=kLoop, calls=%fused_computation.6 | loop fusion | bytes 524288
  57.1 1.7 %constant_dynamic-update-slice_fusion.3.devices = f32[1024,256]{1,0:T(8,128)} fusion(f32[1024,256]{1,0:T(8,128)} %constant_dynamic-update-slice_fusion.4, f32[256,256]{1,0:T(8,128)} %collective-permute-done.8), kind=kLoop, calls=%fused_computation.5 | loop fusion | bytes 524288 | tf_op jit(solution)/shard_map/concatenate | solution.py:571
  58.8 3.4 %pad_maximum_fusion = f32[2592,256]{1,0:T(8,128)} fusion(f32[1024,256]{1,0:T(8,128)} %constant_dynamic-update-slice_fusion.3.devices, f32[784,256]{1,0:T(8,128)} %collective-permute-done.2.right.a_right, f32[784,256]{1,0:T(8,128)} %collective-permute-done.1.left.a_left), kind=kLoop, calls=%fused_computation | loop fusion | flops 1327104 | bytes 5308416 | tf_op jit(solution)/shard_map/concatenate | solution.py:579
  62.3 3.2 %collective-permute-start.13 = (f32[2592,256]{1,0:T(8,128)}, f32[2592,256]{1,0:T(8,128)}, u32[]{:S(2)}, u32[]{:S(2)}) collective-permute-start(f32[2592,256]{1,0:T(8,128)} %pad_maximum_fusion), channel_id=1, source_target_pairs={{0,8},{8,0},{16,24},{24,16},{1,9},{9,1},{17,25},{25,17},{2,10},{10... | collective-permute-start | bytes 7962632 | tf_op jit(solution)/shard_map/ppermute | solution.py:580
  65.4 3.2 %collective-permute-start.11 = (f32[784,256]{1,0:T(8,128)}, f32[784,256]{1,0:T(8,128)}, u32[]{:S(2)}, u32[]{:S(2)}) collective-permute-start(f32[784,256]{1,0:T(8,128)} %collective-permute-done.1.left.a_left), channel_id=1, source_target_pairs={{8,16},{16,8},{9,17},{17,9},{10,18},{18,10},{11,19},{19,11},{12,20... | collective-permute-start | bytes 2408456 | tf_op jit(solution)/shard_map/ppermute | solution.py:577
  68.7 2.3 %collective-permute-start.12 = (f32[784,256]{1,0:T(8,128)}, f32[784,256]{1,0:T(8,128)}, u32[]{:S(2)}, u32[]{:S(2)}) collective-permute-start(f32[784,256]{1,0:T(8,128)} %collective-permute-done.2.right.a_right), channel_id=1, source_target_pairs={{8,16},{16,8},{9,17},{17,9},{10,18},{18,10},{11,19},{19,11},{12,20... | collective-permute-start | bytes 2408456 | tf_op jit(solution)/shard_map/ppermute | solution.py:578
  71.1 1.5 %collective-permute-start.9 = (f32[512,256]{1,0:T(8,128)}, f32[512,256]{1,0:T(8,128)}, u32[]{:S(2)}, u32[]{:S(2)}) collective-permute-start(f32[512,256]{1,0:T(8,128)} %get-tuple-element.47), channel_id=1, source_target_pairs={{0,1},{1,2},{2,3},{3,4},{4,5},{5,6},{6,7},{7,0},{8,9},{9,10},{10,1... | collective-permute-start | bytes 1572872 | tf_op jit(solution)/shard_map/ppermute | solution.py:575
  72.5 7.0 %lon.1.before = f32[4,512,256]{2,1,0:T(8,128)} custom-call(s32[4,9]{1,0:T(4,128)} %bitcast.21, f32[4,8,512]{2,1,0:T(8,128)} %get-tuple-element.34.place8, f32[784,256]{1,0:T(8,128)} %collective-permute-done.1.left.a_left, f32[784,256]{1,0:T(8,128)} %collective-permute-done.2.right.a_right, f32[4,512,256]{2,1,0:T(8,128)} %lat.1.before), custom_call_target="tpu_custom_call", output_to_operand_aliasing={{}: (4, {})} | custom-call | flops 20000000000 | bytes 4000000 | tf_op jit(solution)/shard_map/lon/pallas_call | solution.py:334
  79.5 7.1 %far.1.partial = f32[256,256]{1,0:T(8,128)} custom-call(s32[4,9]{1,0:T(4,128)} %bitcast.22, bf16[4,36,64,64]{3,2,1,0:T(8,128)(2,1)} %bitcast.11, f32[784,256]{1,0:T(8,128)} %get-tuple-element.35.msg.own, f32[784,256]{1,0:T(8,128)} %collective-permute-done.1.left.a_left, f32[784,256]{1,0:T(8,128)} %collective-permute-done.2.right.a_right, ...), custom_call_target="tpu_custom_call" | custom-call | flops 1000 | bytes 1000 | tf_op jit(solution)/shard_map/far/pallas_call | solution.py:465
  86.6 1.5 %collective-permute-done.12.right_y = f32[784,256]{1,0:T(8,128)} collective-permute-done((f32[784,256]{1,0:T(8,128)}, f32[784,256]{1,0:T(8,128)}, u32[]{:S(2)}, u32[]{:S(2)}) %collective-permute-start.12) | collective-permute-done | bytes 802848 | tf_op jit(solution)/shard_map/ppermute | solution.py:578
  88.1 9.2 %down.1.before = f32[4,512,256]{2,1,0:T(8,128)} custom-call(s32[4,9]{1,0:T(4,128)} %bitcast.23, f32[4,8,512]{2,1,0:T(8,128)} %get-tuple-element.34.place8, bf16[4,36,64,64]{3,2,1,0:T(8,128)(2,1)} %bitcast.12, f32[784,256]{1,0:T(8,128)} %collective-permute-done.11.left_y, f32[784,256]{1,0:T(8,128)} %collective-permute-done.12.right_y, ...), custom_call_target="tpu_custom_call", output_to_operand_aliasing={{}: (7, {})} | custom-call | flops 1000 | bytes 1000 | tf_op jit(solution)/shard_map/down/pallas_call | solution.py:334
  97.4 0.1 collective-permute-start.14
  97.4 0.5 collective-permute-start.15
  97.9 1.7 %collective-permute-done.14.left_c = f32[512,256]{1,0:T(8,128)} collective-permute-done((f32[512,256]{1,0:T(8,128)}, f32[512,256]{1,0:T(8,128)}, u32[]{:S(2)}, u32[]{:S(2)}) %collective-permute-start.14) | collective-permute-done | bytes 524320 | tf_op jit(solution)/shard_map/ppermute | solution.py:618
  99.7 0.7 collective-permute-done.15.right_c
  100.4 7.2 %last.1 = f32[4,512,256]{2,1,0:T(8,128)} custom-call(s32[4,9]{1,0:T(4,128)} %bitcast.24, f32[4,8,512]{2,1,0:T(8,128)} %get-tuple-element.34.place8, f32[784,256]{1,0:T(8,128)} %collective-permute-done.1.left.a_left, f32[784,256]{1,0:T(8,128)} %collective-permute-done.2.right.a_right, ...), custom_call_target="tpu_custom_call", output_to_operand_aliasing={{}: (9, {})} | custom-call | flops 20000000000 | bytes 4000000 | tf_op jit(solution)/shard_map/last/pallas_call | solution.py:334
  (17 shorter events, 0.1 us)
Async XLA Ops:
  5.7 12.1 %collective-permute-start = (f32[1296,256]{1,0:T(8,128)}, f32[1296,256]{1,0:T(8,128)}, u32[]{:S(2)}, u32[]{:S(2)}) collective-permute-start(f32[1296,256]{1,0:T(8,128)} %get-tuple-element.32), channel_id=1, source_target_pairs={{0,8},{8,0},{16,24},{24,16},{1,9},{9,1},{17,25},{25,17},{2,10},{10... | collective-permute-start | bytes 3981320 | tf_op jit(solution)/shard_map/ppermute | solution.py:555
  6.5 8.5 %collective-permute-start.3 = (f32[64,256]{1,0:T(8,128)}, f32[64,256]{1,0:T(8,128)S(1)}, u32[]{:S(2)}, u32[]{:S(2)}) collective-permute-start(f32[64,256]{1,0:T(8,128)} %get-tuple-element.39), channel_id=1, source_target_pairs={{0,1},{1,0},{2,3},{3,2},{4,5},{5,4},{6,7},{7,6},{8,9},{9,8},{10,11... | collective-permute-start | bytes 196616 | tf_op jit(solution)/shard_map/ppermute | solution.py:554
  7.7 21.8 %collective-permute-start.4 = (f32[1296,256]{1,0:T(8,128)}, f32[1296,256]{1,0:T(8,128)}, u32[]{:S(2)}, u32[]{:S(2)}) collective-permute-start(f32[1296,256]{1,0:T(8,128)} %get-tuple-element.40), channel_id=1, source_target_pairs={{8,16},{16,8},{9,17},{17,9},{10,18},{18,10},{11,19},{19,11},{12,20... | collective-permute-start | bytes 3981320 | tf_op jit(solution)/shard_map/ppermute | solution.py:556
  11.1 47.8 %collective-permute-start.1 = (f32[784,256]{1,0:T(8,128)}, f32[784,256]{1,0:T(8,128)}, u32[]{:S(2)}, u32[]{:S(2)}) collective-permute-start(f32[784,256]{1,0:T(8,128)} %get-tuple-element.35.msg.own), channel_id=1, source_target_pairs={{0,1},{1,2},{2,3},{3,4},{4,5},{5,6},{6,7},{7,0},{8,9},{9,10},{10,1... | collective-permute-start | bytes 2408456 | tf_op jit(solution)/shard_map/ppermute | solution.py:558
  11.4 47.4 %collective-permute-start.2 = (f32[784,256]{1,0:T(8,128)}, f32[784,256]{1,0:T(8,128)}, u32[]{:S(2)}, u32[]{:S(2)}) collective-permute-start(f32[784,256]{1,0:T(8,128)} %get-tuple-element.36), channel_id=1, source_target_pairs={{0,7},{1,0},{2,1},{3,2},{4,3},{5,4},{6,5},{7,6},{8,15},{9,8},{10,9... | collective-permute-start | bytes 2408456 | tf_op jit(solution)/shard_map/ppermute | solution.py:559
  16.5 13.0 %collective-permute-start.5 = (f32[128,256]{1,0:T(8,128)}, f32[128,256]{1,0:T(8,128)}, u32[]{:S(2)}, u32[]{:S(2)}) collective-permute-start(f32[128,256]{1,0:T(8,128)} %pad_maximum_fusion.1), channel_id=1, source_target_pairs={{0,16},{8,24},{16,0},{24,8},{1,17},{9,25},{17,1},{25,9},{2,18},{10... | collective-permute-start | bytes 393224 | tf_op jit(solution)/shard_map/ppermute | solution.py:561
  17.1 0.7 copy-start
  31.1 10.6 %collective-permute-start.6 = (f32[256,256]{1,0:T(8,128)}, f32[256,256]{1,0:T(8,128)}, u32[]{:S(2)}, u32[]{:S(2)}) collective-permute-start(f32[256,256]{1,0:T(8,128)} %get-tuple-element.59), channel_id=1, source_target_pairs={{0,2},{1,3},{2,4},{3,5},{4,6},{5,7},{6,0},{7,1},{8,10},{9,11},{10,... | collective-permute-start | bytes 786440 | tf_op jit(solution)/shard_map/ppermute | solution.py:567
  31.1 24.3 %collective-permute-start.7 = (f32[256,256]{1,0:T(8,128)}, f32[256,256]{1,0:T(8,128)}, u32[]{:S(2)}, u32[]{:S(2)}) collective-permute-start(f32[256,256]{1,0:T(8,128)} %get-tuple-element.59), channel_id=1, source_target_pairs={{0,4},{1,5},{2,6},{3,7},{4,0},{5,1},{6,2},{7,3},{8,12},{9,13},{10,... | collective-permute-start | bytes 786440 | tf_op jit(solution)/shard_map/ppermute | solution.py:567
  34.2 22.9 %collective-permute-start.8 = (f32[256,256]{1,0:T(8,128)}, f32[256,256]{1,0:T(8,128)}, u32[]{:S(2)}, u32[]{:S(2)}) collective-permute-start(f32[256,256]{1,0:T(8,128)} %get-tuple-element.59), channel_id=1, source_target_pairs={{0,6},{1,7},{2,0},{3,1},{4,2},{5,3},{6,4},{7,5},{8,14},{9,15},{10,... | collective-permute-start | bytes 786440 | tf_op jit(solution)/shard_map/ppermute | solution.py:567
  62.3 17.3 %collective-permute-start.13 = (f32[2592,256]{1,0:T(8,128)}, f32[2592,256]{1,0:T(8,128)}, u32[]{:S(2)}, u32[]{:S(2)}) collective-permute-start(f32[2592,256]{1,0:T(8,128)} %pad_maximum_fusion), channel_id=1, source_target_pairs={{0,8},{8,0},{16,24},{24,16},{1,9},{9,1},{17,25},{25,17},{2,10},{10... | collective-permute-start | bytes 7962632 | tf_op jit(solution)/shard_map/ppermute | solution.py:580
  65.4 21.2 %collective-permute-start.11 = (f32[784,256]{1,0:T(8,128)}, f32[784,256]{1,0:T(8,128)}, u32[]{:S(2)}, u32[]{:S(2)}) collective-permute-start(f32[784,256]{1,0:T(8,128)} %collective-permute-done.1.left.a_left), channel_id=1, source_target_pairs={{8,16},{16,8},{9,17},{17,9},{10,18},{18,10},{11,19},{19,11},{12,20... | collective-permute-start | bytes 2408456 | tf_op jit(solution)/shard_map/ppermute | solution.py:577
  68.7 19.4 %collective-permute-start.12 = (f32[784,256]{1,0:T(8,128)}, f32[784,256]{1,0:T(8,128)}, u32[]{:S(2)}, u32[]{:S(2)}) collective-permute-start(f32[784,256]{1,0:T(8,128)} %collective-permute-done.2.right.a_right), channel_id=1, source_target_pairs={{8,16},{16,8},{9,17},{17,9},{10,18},{18,10},{11,19},{19,11},{12,20... | collective-permute-start | bytes 2408456 | tf_op jit(solution)/shard_map/ppermute | solution.py:578
  71.0 26.3 %collective-permute-start.10 = (f32[512,256]{1,0:T(8,128)}, f32[512,256]{1,0:T(8,128)}, u32[]{:S(2)}, u32[]{:S(2)}) collective-permute-start(f32[512,256]{1,0:T(8,128)} %get-tuple-element.48), channel_id=1, source_target_pairs={{0,7},{1,0},{2,1},{3,2},{4,3},{5,4},{6,5},{7,6},{8,15},{9,8},{10,9... | collective-permute-start | bytes 1572872 | tf_op jit(solution)/shard_map/ppermute | solution.py:576
  71.1 26.3 %collective-permute-start.9 = (f32[512,256]{1,0:T(8,128)}, f32[512,256]{1,0:T(8,128)}, u32[]{:S(2)}, u32[]{:S(2)}) collective-permute-start(f32[512,256]{1,0:T(8,128)} %get-tuple-element.47), channel_id=1, source_target_pairs={{0,1},{1,2},{2,3},{3,4},{4,5},{5,6},{6,7},{7,0},{8,9},{9,10},{10,1... | collective-permute-start | bytes 1572872 | tf_op jit(solution)/shard_map/ppermute | solution.py:575
  97.4 2.3 %collective-permute-start.14 = (f32[512,256]{1,0:T(8,128)}, f32[512,256]{1,0:T(8,128)}, u32[]{:S(2)}, u32[]{:S(2)}) collective-permute-start(f32[512,256]{1,0:T(8,128)} %collective-permute-done.9.left), channel_id=1, source_target_pairs={{0,8},{8,0},{16,24},{24,16},{1,9},{9,1},{17,25},{25,17},{2,10},{10... | collective-permute-start | bytes 1572872 | tf_op jit(solution)/shard_map/ppermute | solution.py:618
  97.4 3.0 %collective-permute-start.15 = (f32[512,256]{1,0:T(8,128)}, f32[512,256]{1,0:T(8,128)}, u32[]{:S(2)}, u32[]{:S(2)}) collective-permute-start(f32[512,256]{1,0:T(8,128)} %collective-permute-done.10.right), channel_id=1, source_target_pairs={{0,8},{8,0},{16,24},{24,16},{1,9},{9,1},{17,25},{25,17},{2,10},{10... | collective-permute-start | bytes 1572872 | tf_op jit(solution)/shard_map/ppermute | solution.py:619
